TPU v7x, 512 devices: a whole 4x8x8 slice. The times are simulated.
512 devices in a mesh: ctx: 32 (over x, z), dp: 16 (over y, core).
Axes of the slice: x: 4, y: 8, z: 8, core: 2. Of those that a mesh axis runs over, the one named last changes fastest.
Arguments:
- queries: bfloat16 [65536, 4096], P(('dp', 'ctx')), parts along dimension 0, may hold values from -5 to 5
- keys: bfloat16 [65536, 512], P(('dp', 'ctx')), parts along dimension 0, may hold values from -5 to 5
- values: bfloat16 [65536, 512], P(('dp', 'ctx')), parts along dimension 0, may hold values from -6 to 6
- output_gradient: bfloat16 [65536, 4096], P(('dp', 'ctx')), parts along dimension 0, may hold values from -6 to 6
- doc_lengths: int32 [336], P('dp'), parts along dimension 0, may hold values from 1 to 384, 4096 in all
- span_order: int32 [1024], P('dp'), parts along dimension 0, may hold values from 0 to 63, each once
Outputs:
- attended: bfloat16 [65536, 4096], P(('dp', 'ctx')), parts along dimension 0
- grad_queries: bfloat16 [65536, 4096], P(('dp', 'ctx')), parts along dimension 0
- grad_keys: bfloat16 [65536, 512], P(('dp', 'ctx')), parts along dimension 0
- grad_values: bfloat16 [65536, 512], P(('dp', 'ctx')), parts along dimension 0
There are 16 independent parts, one for each index of `dp`. A program takes and returns all parts, laid end to end along the dimension named above; each array names one. Nothing has to cross between parts.
Inputs may be any that keep to these rules, and one draw needn't show every extreme that they name: `doc_lengths`: the largest length is exactly 384. `span_order`: a permutation.
All inputs are finite; a program needn't handle non-finite values.
Results may differ from a plain program's by a relative error of at most 0.0071.
Values may be sent and summed in bfloat16 or wider, within the bound.
A program may use at most 64 MiB of HBM per device.

v0:
```python
import jax
import jax.numpy as jnp
from jax import lax
from jax.sharding import PartitionSpec as P

HEAD_DIMENSION = 128
QUERY_HEADS = 32
KEY_VALUE_HEADS = 4
MOST = 384


def document_ids(doc_lengths, count):
    doc_ends = jnp.cumsum(doc_lengths)
    places = jnp.arange(count, dtype=jnp.int32)
    return jnp.sum((places[:, None] >= doc_ends[None, :]).astype(jnp.int32), axis=1)


def to_position(token_row_count, span_order):
    pieces = span_order.shape[0]
    blocks = token_row_count.reshape(
        pieces, token_row_count.shape[0] // pieces, token_row_count.shape[1]
    )
    inverse = (
        jnp.zeros((pieces,), jnp.int32).at[span_order].set(jnp.arange(pieces, dtype=jnp.int32))
    )
    return blocks[inverse].reshape(token_row_count.shape)


def to_storage(token_row_count, span_order):
    pieces = span_order.shape[0]
    blocks = token_row_count.reshape(
        pieces, token_row_count.shape[0] // pieces, token_row_count.shape[1]
    )
    return blocks[span_order].reshape(token_row_count.shape)


def padded(token_row_count, reach, fill):
    front = jnp.full((reach,) + token_row_count.shape[1:], fill, token_row_count.dtype)
    return jnp.concatenate([front, token_row_count], axis=0)


def window_probs(query_rows, key_window, docs, doc_pad, start, block, reach):
    width = query_rows.shape[1]
    query_docs = lax.dynamic_slice_in_dim(docs, start, block)
    key_docs = lax.dynamic_slice_in_dim(doc_pad, start, block + reach)
    query_place = start + jnp.arange(block, dtype=jnp.int32)
    key_place = start - reach + jnp.arange(block + reach, dtype=jnp.int32)
    visible = (key_docs[None, :] == query_docs[:, None]) & (
        key_place[None, :] <= query_place[:, None]
    )
    scores = jnp.dot(query_rows, key_window.T, preferred_element_type=jnp.float32) * width ** (-0.5)
    scores = jnp.where(visible, scores, -jnp.inf)
    peak = jnp.max(scores, axis=1, keepdims=True)
    weights = jnp.exp(scores - peak)
    return weights / jnp.sum(weights, axis=1, keepdims=True)


def head_forward(query, keys, values, docs, block, reach):
    total_count = query.shape[0]
    key_pad = padded(keys, reach, 0)
    value_pad = padded(values, reach, 0)
    doc_pad = padded(docs, reach, -1)

    def one_block(block_index, result):
        start = (block_index * block).astype(jnp.int32)
        query_rows = lax.dynamic_slice_in_dim(query, start, block)
        key_window = lax.dynamic_slice_in_dim(key_pad, start, block + reach)
        value_window = lax.dynamic_slice_in_dim(value_pad, start, block + reach)
        probs = window_probs(query_rows, key_window, docs, doc_pad, start, block, reach).astype(
            jnp.bfloat16
        )
        mixed_layout = jnp.dot(probs, value_window, preferred_element_type=jnp.float32).astype(
            jnp.bfloat16
        )
        return lax.dynamic_update_slice_in_dim(result, mixed_layout, start, 0)

    return lax.fori_loop(0, total_count // block, one_block, jnp.zeros(query.shape, jnp.bfloat16))


def head_backward(query, keys, values, grad_out, docs, block, reach):
    total_count, width = query.shape
    key_pad = padded(keys, reach, 0)
    value_pad = padded(values, reach, 0)
    doc_pad = padded(docs, reach, -1)

    def one_block(block_index, carry):
        query_gradient, key_gradient, value_gradient = carry
        start = (block_index * block).astype(jnp.int32)
        query_rows = lax.dynamic_slice_in_dim(query, start, block)
        grad_rows = lax.dynamic_slice_in_dim(grad_out, start, block)
        key_window = lax.dynamic_slice_in_dim(key_pad, start, block + reach)
        value_window = lax.dynamic_slice_in_dim(value_pad, start, block + reach)
        probs = window_probs(query_rows, key_window, docs, doc_pad, start, block, reach)
        probs_low = probs.astype(jnp.bfloat16)
        grad_probs = jnp.dot(grad_rows, value_window.T, preferred_element_type=jnp.float32)
        centre = jnp.sum(probs * grad_probs, axis=1, keepdims=True)
        grad_scores = (probs * (grad_probs - centre) * width ** (-0.5)).astype(jnp.bfloat16)
        query_part = jnp.dot(grad_scores, key_window, preferred_element_type=jnp.float32).astype(
            jnp.bfloat16
        )
        key_part = jnp.dot(grad_scores.T, query_rows, preferred_element_type=jnp.float32)
        value_part = jnp.dot(probs_low.T, grad_rows, preferred_element_type=jnp.float32)
        query_gradient = lax.dynamic_update_slice_in_dim(query_gradient, query_part, start, 0)
        old_k = lax.dynamic_slice_in_dim(key_gradient, start, block + reach)
        old_v = lax.dynamic_slice_in_dim(value_gradient, start, block + reach)
        key_gradient = lax.dynamic_update_slice_in_dim(key_gradient, old_k + key_part, start, 0)
        value_gradient = lax.dynamic_update_slice_in_dim(
            value_gradient, old_v + value_part, start, 0
        )
        return (query_gradient, key_gradient, value_gradient)

    start_carry = (
        jnp.zeros(query.shape, jnp.bfloat16),
        jnp.zeros((total_count + reach, width), jnp.float32),
        jnp.zeros((total_count + reach, width), jnp.float32),
    )
    query_gradient, key_gradient, value_gradient = lax.fori_loop(
        0, total_count // block, one_block, start_carry
    )
    return (query_gradient, key_gradient[reach:], value_gradient[reach:])


def local(queries, keys, values, output_gradient, doc_lengths, span_order):
    devices = lax.axis_size("ctx")
    token_rows = queries.shape[0]
    total_count = token_rows * devices
    head_group = QUERY_HEADS // KEY_VALUE_HEADS
    own_heads = QUERY_HEADS // devices
    repeat_factor = max(1, head_group // own_heads)
    block = min(512, total_count)

    def spread(token_row_count):
        wide_layout = jnp.broadcast_to(
            token_row_count.reshape(token_rows, KEY_VALUE_HEADS, 1, HEAD_DIMENSION),
            (token_rows, KEY_VALUE_HEADS, repeat_factor, HEAD_DIMENSION),
        )
        return wide_layout.reshape(token_rows, KEY_VALUE_HEADS * repeat_factor * HEAD_DIMENSION)

    key_spread = spread(keys)
    value_spread = spread(values)
    query_all, key_all, value_all = (
        lax.all_to_all(queries, "ctx", split_axis=1, concat_axis=0, tiled=True),
        lax.all_to_all(key_spread, "ctx", split_axis=1, concat_axis=0, tiled=True),
        lax.all_to_all(value_spread, "ctx", split_axis=1, concat_axis=0, tiled=True),
    )
    docs = document_ids(doc_lengths, total_count)
    query_pos = to_position(query_all, span_order)
    key_pos = to_position(key_all, span_order)
    value_pos = to_position(value_all, span_order)
    mixed_heads = head_forward(query_pos, key_pos, value_pos, docs, block, MOST)
    mixed_store = to_storage(mixed_heads, span_order)
    grad_all = lax.all_to_all(output_gradient, "ctx", split_axis=1, concat_axis=0, tiled=True)
    grad_pos = to_position(grad_all, span_order)
    key_sums = [jnp.zeros((total_count, HEAD_DIMENSION), jnp.float32)]
    value_sums = [jnp.zeros((total_count, HEAD_DIMENSION), jnp.float32)]
    slot = 0 // head_group
    query_gradient, key_gradient, value_gradient = head_backward(
        query_pos, key_pos, value_pos, grad_pos, docs, block, MOST
    )
    key_sums[slot] = key_gradient
    value_sums[slot] = value_gradient
    query_store = to_storage(query_gradient, span_order)
    key_store = to_storage(key_sums[0], span_order)
    value_store = to_storage(value_sums[0], span_order)
    mixed_back, query_back = (
        lax.all_to_all(mixed_store, "ctx", split_axis=0, concat_axis=1, tiled=True),
        lax.all_to_all(query_store, "ctx", split_axis=0, concat_axis=1, tiled=True),
    )
    key_parts, value_parts = (
        lax.all_to_all(key_store, "ctx", split_axis=0, concat_axis=1, tiled=True),
        lax.all_to_all(value_store, "ctx", split_axis=0, concat_axis=1, tiled=True),
    )

    def fold_slots(partial_pieces):
        reduced_pieces = jnp.sum(
            partial_pieces.reshape(token_rows, KEY_VALUE_HEADS, repeat_factor, HEAD_DIMENSION),
            axis=2,
        )
        return reduced_pieces.reshape(token_rows, KEY_VALUE_HEADS * HEAD_DIMENSION).astype(
            jnp.bfloat16
        )

    key_back = fold_slots(key_parts)
    value_back = fold_slots(value_parts)
    return (mixed_back, query_back, key_back, value_back)


def solution(mesh):
    return jax.shard_map(
        local,
        mesh=mesh,
        in_specs=(
            P(("dp", "ctx"), None),
            P(("dp", "ctx"), None),
            P(("dp", "ctx"), None),
            P(("dp", "ctx"), None),
            P("dp"),
            P("dp"),
        ),
        out_specs=(
            P(("dp", "ctx"), None),
            P(("dp", "ctx"), None),
            P(("dp", "ctx"), None),
            P(("dp", "ctx"), None),
        ),
        check_vma=False,
    )
```

profile of v0, /device:TPU:56, one launch (start us, length us, event | category | flops | bytes accessed | tf_op | source)
XLA Modules:
  0.0 421.8 jit_solution(6899290610117371720)
XLA Ops:
  2.8 13.2 %all-to-all-start.1 = ((bf16[128,32,128]{2,0,1:T(8,128)(2,1)}), bf16[128,32,128]{2,0,1:T(8,128)(2,1)S(1)}, u32[]{:S(2)}, u32[]{:S(2)}) async-start(bf16[128,32,128]{2,0,1:T(8,128)(2,1)} %bitcast.5), calls=%async_computation.1 | async-start | bytes 2097152 | tf_op jit(solution)/shard_map/all_to_all | solution.py:143
  16.0 28.6 %all-to-all-done.1 = bf16[128,32,128]{2,0,1:T(8,128)(2,1)S(1)} async-done(((bf16[128,32,128]{2,0,1:T(8,128)(2,1)}), bf16[128,32,128]{2,0,1:T(8,128)(2,1)S(1)}, u32[]{:S(2)}, u32[]{:S(2)}) %all-to-all-start.1) | async-done | bytes 1048608 | tf_op jit(solution)/shard_map/all_to_all | solution.py:143
  45.8 5.1 %all-to-all-start.2 = ((bf16[128,32,128]{2,0,1:T(8,128)(2,1)}), bf16[128,32,128]{2,0,1:T(8,128)(2,1)S(1)}, u32[]{:S(2)}, u32[]{:S(2)}) async-start(bf16[128,32,128]{2,0,1:T(8,128)(2,1)} %bitcast.9), calls=%async_computation.2 | async-start | bytes 2097152 | tf_op jit(solution)/shard_map/all_to_all | solution.py:144
  52.2 27.0 %all-to-all-done.2 = bf16[128,32,128]{2,0,1:T(8,128)(2,1)S(1)} async-done(((bf16[128,32,128]{2,0,1:T(8,128)(2,1)}), bf16[128,32,128]{2,0,1:T(8,128)(2,1)S(1)}, u32[]{:S(2)}, u32[]{:S(2)}) %all-to-all-start.2) | async-done | bytes 1048608 | tf_op jit(solution)/shard_map/all_to_all | solution.py:144
  79.2 4.9 %all-to-all-start = ((bf16[128,32,128]{0,2,1:T(8,128)(2,1)}), bf16[128,32,128]{0,2,1:T(8,128)(2,1)S(1)}, u32[]{:S(2)}, u32[]{:S(2)}) async-start(bf16[128,32,128]{0,2,1:T(8,128)(2,1)} %bitcast.71), calls=%async_computation | async-start | bytes 2097152 | tf_op jit(solution)/shard_map/all_to_all | solution.py:142
  84.1 2.3 copy.57
  86.4 26.0 %all-to-all-done = bf16[128,32,128]{0,2,1:T(8,128)(2,1)S(1)} async-done(((bf16[128,32,128]{0,2,1:T(8,128)(2,1)}), bf16[128,32,128]{0,2,1:T(8,128)(2,1)S(1)}, u32[]{:S(2)}, u32[]{:S(2)}) %all-to-all-start) | async-done | bytes 1048608 | tf_op jit(solution)/shard_map/all_to_all | solution.py:142
  112.4 5.0 %all-to-all-start.4 = ((bf16[128,32,128]{0,2,1:T(8,128)(2,1)}), bf16[128,32,128]{0,2,1:T(8,128)(2,1)}, u32[]{:S(2)}, u32[]{:S(2)}) async-start(bf16[128,32,128]{0,2,1:T(8,128)(2,1)} %bitcast.69), calls=%async_computation.4 | async-start | bytes 2097152 | tf_op jit(solution)/shard_map/all_to_all | solution.py:152
  120.2 1.6 copy.53
  121.9 1.7 gather_fusion
  123.5 22.2 %all-to-all-done.4 = bf16[128,32,128]{0,2,1:T(8,128)(2,1)} async-done(((bf16[128,32,128]{0,2,1:T(8,128)(2,1)}), bf16[128,32,128]{0,2,1:T(8,128)(2,1)}, u32[]{:S(2)}, u32[]{:S(2)}) %all-to-all-start.4) | async-done | bytes 1048608 | tf_op jit(solution)/shard_map/all_to_all | solution.py:152
  145.7 1.6 copy.58
  147.3 1.7 gather_fusion.4
  153.0 80.8 %while.35 = (s32[]{:T(128)}, bf16[4096,128]{1,0:T(8,128)(2,1)S(1)}, f32[4480,128]{1,0:T(8,128)S(1)}, f32[4480,128]{1,0:T(8,128)}, s32[4480]{0:T(1024)S(1)}, /*in...) while((s32[]{:T(128)}, bf16[4096,128]{1,0:T(8,128)(2,1)S(1)}, ...), condition=%wide.region_11.12_spmd, body=%wide.region_7.11_spmd.sunk | while | flops 597131136 | bytes 18827040 | solution.py:117
  153.2 1.7 fusion.60
  155.4 2.6 fusion.64
  158.0 1.7 multiply_reduce_fusion.2
  163.3 1.7 fusion.60
  165.5 2.6 fusion.64
  168.1 1.7 multiply_reduce_fusion.2
  173.4 1.7 fusion.60
  175.6 2.6 fusion.64
  178.2 1.7 multiply_reduce_fusion.2
  183.5 1.7 fusion.60
  185.7 2.6 fusion.64
  188.3 1.7 multiply_reduce_fusion.2
  193.6 1.7 fusion.60
  195.8 2.6 fusion.64
  198.4 1.7 multiply_reduce_fusion.2
  203.7 1.7 fusion.60
  205.9 2.6 fusion.64
  208.5 1.7 multiply_reduce_fusion.2
  213.8 1.7 fusion.60
  216.0 2.6 fusion.64
  218.6 1.7 multiply_reduce_fusion.2
  223.9 1.7 fusion.60
  226.1 2.6 fusion.64
  228.7 1.7 multiply_reduce_fusion.2
  233.8 1.7 gather_fusion.5
  235.5 5.0 %all-to-all-start.5 = ((bf16[32,128,128]{2,1,0:T(8,128)(2,1)}), bf16[32,128,128]{2,1,0:T(8,128)(2,1)}, u32[]{:S(2)}, u32[]{:S(2)}) async-start(bf16[32,128,128]{2,1,0:T(8,128)(2,1)} %bitcast.22), calls=%async_computation.5 | async-start | bytes 2097152 | tf_op jit(solution)/shard_map/all_to_all | solution.py:167
  240.7 31.1 %while.34 = (s32[]{:T(128)}, bf16[4096,128]{1,0:T(8,128)(2,1)S(1)}, s32[4480]{0:T(1024)S(1)}, s32[4096]{0:T(1024)S(1)}, bf16[4096,128]{1,0:T(8,128)(2,1)}, /*ind...) while((s32[]{:T(128)}, bf16[4096,128]{1,0:T(8,128)(2,1)S(1)}, ...), condition=%wide.region_6.7_spmd, body=%wide.region_3.0_spmd.sunk | while | flops 239993216 | bytes 6264560 | solution.py:77
  240.9 1.7 fusion.51
  244.7 1.7 fusion.51
  248.6 1.7 fusion.51
  252.5 1.7 fusion.51
  254.7 1.6 fusion.53
  256.4 1.7 fusion.51
  260.3 1.7 fusion.51
  262.4 1.6 fusion.53
  264.2 1.7 fusion.51
  268.1 1.7 fusion.51
  271.8 1.7 gather_fusion.3
  273.5 9.9 %all-to-all-start.3 = ((bf16[32,128,128]{2,1,0:T(8,128)(2,1)}), bf16[32,128,128]{2,1,0:T(8,128)(2,1)S(1)}, u32[]{:S(2)}, u32[]{:S(2)}) async-start(bf16[32,128,128]{2,1,0:T(8,128)(2,1)} %bitcast.14), calls=%async_computation.3 | async-start | bytes 2097152 | tf_op jit(solution)/shard_map/all_to_all | solution.py:166
  284.8 3.6 gather_fusion.6
  288.4 22.5 %all-to-all-done.3 = bf16[32,128,128]{2,1,0:T(8,128)(2,1)S(1)} async-done(((bf16[32,128,128]{2,1,0:T(8,128)(2,1)}), bf16[32,128,128]{2,1,0:T(8,128)(2,1)S(1)}, u32[]{:S(2)}, u32[]{:S(2)}) %all-to-all-start.3) | async-done | bytes 1048608 | tf_op jit(solution)/shard_map/all_to_all | solution.py:166
  310.9 5.2 %all-to-all-start.6 = ((f32[32,128,128]{2,1,0:T(8,128)}), f32[32,128,128]{2,1,0:T(8,128)}, u32[]{:S(2)}, u32[]{:S(2)}) async-start(f32[32,128,128]{2,1,0:T(8,128)} %bitcast.57), calls=%async_computation.6 | async-start | bytes 4194304 | tf_op jit(solution)/shard_map/all_to_all | solution.py:170
  317.6 3.6 gather_fusion.7
  321.2 44.1 %all-to-all-done.6 = f32[32,128,128]{2,1,0:T(8,128)} async-done(((f32[32,128,128]{2,1,0:T(8,128)}), f32[32,128,128]{2,1,0:T(8,128)}, u32[]{:S(2)}, u32[]{:S(2)}) %all-to-all-start.6) | async-done | bytes 2097184 | tf_op jit(solution)/shard_map/all_to_all | solution.py:170
  365.3 5.9 %all-to-all-start.7 = ((f32[32,128,128]{2,1,0:T(8,128)}), f32[32,128,128]{2,1,0:T(8,128)S(1)}, u32[]{:S(2)}, u32[]{:S(2)}) async-start(f32[32,128,128]{2,1,0:T(8,128)} %bitcast.31), calls=%async_computation.7 | async-start | bytes 4194304 | tf_op jit(solution)/shard_map/all_to_all | solution.py:171
  371.2 2.3 copy.59
  373.4 2.3 copy.63
  377.0 2.3 copy.62
  379.2 1.7 bitcast_reduce_fusion.1
  381.9 38.9 %all-to-all-done.7 = f32[32,128,128]{2,1,0:T(8,128)S(1)} async-done(((f32[32,128,128]{2,1,0:T(8,128)}), f32[32,128,128]{2,1,0:T(8,128)S(1)}, u32[]{:S(2)}, u32[]{:S(2)}) %all-to-all-start.7) | async-done | bytes 2097184 | tf_op jit(solution)/shard_map/all_to_all | solution.py:171
  (157 shorter events, 64.1 us)
Async XLA Ops:
  0.6 0.9 copy-start
  0.6 15.3 %copy-start.4 = (bf16[128,512]{1,0:T(8,128)(2,1)S(1)}, bf16[128,512]{1,0:T(8,128)(2,1)}, u32[]{:S(2)}) copy-start(bf16[128,512]{1,0:T(8,128)(2,1)} %param.12) | copy-start | bytes 393220
  2.8 41.8 %all-to-all-start.1 = ((bf16[128,32,128]{2,0,1:T(8,128)(2,1)}), bf16[128,32,128]{2,0,1:T(8,128)(2,1)S(1)}, u32[]{:S(2)}, u32[]{:S(2)}) async-start(bf16[128,32,128]{2,0,1:T(8,128)(2,1)} %bitcast.5), calls=%async_computation.1 | async-start | bytes 2097152 | tf_op jit(solution)/shard_map/all_to_all | solution.py:143
  16.0 34.9 %copy-start.3 = (bf16[128,4096]{1,0:T(8,128)(2,1)S(1)}, bf16[128,4096]{1,0:T(8,128)(2,1)}, u32[]{:S(2)}) copy-start(bf16[128,4096]{1,0:T(8,128)(2,1)} %param.10) | copy-start | bytes 3145732
  45.8 33.4 %all-to-all-start.2 = ((bf16[128,32,128]{2,0,1:T(8,128)(2,1)}), bf16[128,32,128]{2,0,1:T(8,128)(2,1)S(1)}, u32[]{:S(2)}, u32[]{:S(2)}) async-start(bf16[128,32,128]{2,0,1:T(8,128)(2,1)} %bitcast.9), calls=%async_computation.2 | async-start | bytes 2097152 | tf_op jit(solution)/shard_map/all_to_all | solution.py:144
  79.2 33.2 %all-to-all-start = ((bf16[128,32,128]{0,2,1:T(8,128)(2,1)}), bf16[128,32,128]{0,2,1:T(8,128)(2,1)S(1)}, u32[]{:S(2)}, u32[]{:S(2)}) async-start(bf16[128,32,128]{0,2,1:T(8,128)(2,1)} %bitcast.71), calls=%async_computation | async-start | bytes 2097152 | tf_op jit(solution)/shard_map/all_to_all | solution.py:142
  84.1 33.4 %copy-start.5 = (s32[21]{0:T(128)S(1)}, s32[21]{0:T(128)}, u32[]{:S(2)}) copy-start(s32[21]{0:T(128)} %param.14) | copy-start | bytes 256
  84.1 33.6 %copy-start.6 = (s32[64]{0:T(128)S(1)}, s32[64]{0:T(128)}, u32[]{:S(2)}) copy-start(s32[64]{0:T(128)} %param.15) | copy-start | bytes 772
  112.4 6.3 %copy-start.2 = (bf16[128,32,128]{0,2,1:T(8,128)(2,1)}, bf16[128,32,128]{0,2,1:T(8,128)(2,1)S(1)}, u32[]{:S(2)}) copy-start(bf16[128,32,128]{0,2,1:T(8,128)(2,1)S(1)} %all-to-all-done) | copy-start | bytes 3145732
  112.4 33.3 %all-to-all-start.4 = ((bf16[128,32,128]{0,2,1:T(8,128)(2,1)}), bf16[128,32,128]{0,2,1:T(8,128)(2,1)}, u32[]{:S(2)}, u32[]{:S(2)}) async-start(bf16[128,32,128]{0,2,1:T(8,128)(2,1)} %bitcast.69), calls=%async_computation.4 | async-start | bytes 2097152 | tf_op jit(solution)/shard_map/all_to_all | solution.py:152
  235.5 38.0 %all-to-all-start.5 = ((bf16[32,128,128]{2,1,0:T(8,128)(2,1)}), bf16[32,128,128]{2,1,0:T(8,128)(2,1)}, u32[]{:S(2)}, u32[]{:S(2)}) async-start(bf16[32,128,128]{2,1,0:T(8,128)(2,1)} %bitcast.22), calls=%async_computation.5 | async-start | bytes 2097152 | tf_op jit(solution)/shard_map/all_to_all | solution.py:167
  273.5 37.4 %all-to-all-start.3 = ((bf16[32,128,128]{2,1,0:T(8,128)(2,1)}), bf16[32,128,128]{2,1,0:T(8,128)(2,1)S(1)}, u32[]{:S(2)}, u32[]{:S(2)}) async-start(bf16[32,128,128]{2,1,0:T(8,128)(2,1)} %bitcast.14), calls=%async_computation.3 | async-start | bytes 2097152 | tf_op jit(solution)/shard_map/all_to_all | solution.py:166
  310.9 5.2 %copy-start.1 = (f32[4480,128]{1,0:T(8,128)S(1)}, f32[4480,128]{1,0:T(8,128)}, u32[]{:S(2)}) copy-start(f32[4480,128]{1,0:T(8,128)} %get-tuple-element.427) | copy-start | bytes 6881284
  310.9 54.4 %all-to-all-start.6 = ((f32[32,128,128]{2,1,0:T(8,128)}), f32[32,128,128]{2,1,0:T(8,128)}, u32[]{:S(2)}, u32[]{:S(2)}) async-start(f32[32,128,128]{2,1,0:T(8,128)} %bitcast.57), calls=%async_computation.6 | async-start | bytes 4194304 | tf_op jit(solution)/shard_map/all_to_all | solution.py:170
  365.3 55.5 %all-to-all-start.7 = ((f32[32,128,128]{2,1,0:T(8,128)}), f32[32,128,128]{2,1,0:T(8,128)S(1)}, u32[]{:S(2)}, u32[]{:S(2)}) async-start(f32[32,128,128]{2,1,0:T(8,128)} %bitcast.31), calls=%async_computation.7 | async-start | bytes 4194304 | tf_op jit(solution)/shard_map/all_to_all | solution.py:171
where the time goes:
time: 424 us; the launch traced here: 422 us
  waiting for transfers between devices  209 us (49%)
  matrix products  96.5 us (23%)
  starting transfers between devices  54.2 us (13%)
  local copies, waits for them, and re-layouts  45.8 us (11%)
  other arithmetic  14.6 us (3%)
    all_to_all x1, waiting for transfers between devices, local(): lax.all_to_all(key_store, 'ctx', split_axis=0, concat_axis=1, tiled=True)  44.1 us
    all_to_all x1, waiting for transfers between devices, local(): lax.all_to_all(value_store, 'ctx', split_axis=0, concat_axis=1, tiled=True)  38.9 us
    all_to_all x1, waiting for transfers between devices, local(): lax.all_to_all(key_spread, 'ctx', split_axis=1, concat_axis=0, tiled=True)  28.6 us
    all_to_all x1, waiting for transfers between devices, local(): lax.all_to_all(value_spread, 'ctx', split_axis=1, concat_axis=0, tiled=True)  27 us
    dot_general x16, matrix products, window_probs(): jnp.dot(query_rows, key_window.T, preferred_element_type=jnp.float32)  26.8 us
    all_to_all x1, waiting for transfers between devices, local(): lax.all_to_all(queries, 'ctx', split_axis=1, concat_axis=0, tiled=True)  26 us
    all_to_all x1, waiting for transfers between devices, local(): lax.all_to_all(mixed_store, 'ctx', split_axis=0, concat_axis=1, tiled=True)  22.5 us
    all_to_all x1, waiting for transfers between devices, local(): lax.all_to_all(output_gradient, 'ctx', split_axis=1, concat_axis=0, tiled...  22.2 us
  transfers between devices with their start and end apart: 8, of which 7 were waited for; matrix products, arithmetic and copies ran while one was open for 15% of the time, Pallas kernels for 0%

commit v1 on v0

v1 whole, which is shorter than its diff:
```python
import functools

import jax
import jax.numpy as jnp
from jax import lax
from jax.experimental import pallas as pl
from jax.experimental.pallas import tpu as pltpu
from jax.sharding import PartitionSpec as P

HD = 128
QH = 32
KH = 4
GH = QH // KH
C = 64
NB = 7
W = NB * C
NX = 4
GW = GH * HD
LOG2E = 1.4426950408889634
MESH = pl.DeviceIdType.MESH
F32 = jnp.float32
BF16 = jnp.bfloat16


def kernel(
    nz,
    q_ref,
    k_ref,
    v_ref,
    g_ref,
    len_ref,
    span_ref,
    inv_ref,
    o_out,
    gq_out,
    gk_out,
    gv_out,
    kv,
    qx,
    dx,
    ox,
    gx,
    ck,
    cv,
    send_buf,
    recv_buf,
    fin,
    loc_sem,
    xin_send,
    xin_recv,
    zin_send,
    zin_recv,
    xout_send,
    xout_recv,
    zout_send,
    zout_recv,
):
    half = nz // 2
    rows = q_ref.shape[0]
    per = rows // C
    me = lax.axis_index("ctx")
    x = me // nz
    z = lax.rem(me, nz)
    ndoc = len_ref.shape[0]

    def at_x(r):
        return lax.rem(x + r + NX, NX)

    def at_z(r):
        return lax.rem(z + r + nz, nz)

    def dev(xx, zz):
        return {"ctx": xx * nz + zz}

    def cols(g, width):
        return pl.ds(pl.multiple_of(g * width, width), width)

    def pblocks(piece):
        return pl.ds(piece * per, per)

    def prows(piece):
        return pl.ds(pl.multiple_of(piece * rows, rows), rows)

    own = z * NX + x
    local = [
        pltpu.make_async_copy(k_ref.at[:, :, cols(x, HD)], kv.at[0, pblocks(own)], loc_sem.at[0]),
        pltpu.make_async_copy(v_ref.at[:, :, cols(x, HD)], kv.at[1, pblocks(own)], loc_sem.at[1]),
        pltpu.make_async_copy(q_ref.at[:, cols(x, GW)], qx.at[prows(x)], loc_sem.at[2]),
        pltpu.make_async_copy(g_ref.at[:, cols(x, GW)], dx.at[prows(x)], loc_sem.at[3]),
    ]
    for c in local:
        c.start()

    barrier = pltpu.get_barrier_semaphore()
    peers = [dev(at_x(r), z) for r in (1, 2, 3)] + [dev(x, at_z(r)) for r in (1, -1)]
    for p in peers:
        pl.semaphore_signal(barrier, inc=1, device_id=p, device_id_type=MESH)
    pl.semaphore_wait(barrier, len(peers))

    def x_in(a, r):
        g = at_x(r)
        if a < 2:
            src, dst = (k_ref, v_ref)[a].at[:, :, cols(g, HD)], kv.at[a, pblocks(own)]
        else:
            src, dst = (q_ref, g_ref)[a - 2].at[:, cols(g, GW)], (qx, dx)[a - 2].at[prows(x)]
        return pltpu.make_async_remote_copy(
            src_ref=src,
            dst_ref=dst,
            send_sem=xin_send.at[a, r - 1],
            recv_sem=xin_recv.at[a, r - 1],
            device_id=dev(g, z),
            device_id_type=MESH,
        )

    def x_in_wait(a, r):
        src = at_x(-r)
        if a < 2:
            dst = kv.at[a, pblocks(z * NX + src)]
        else:
            dst = (qx, dx)[a - 2].at[prows(src)]
        pltpu.make_async_remote_copy(
            src_ref=dst,
            dst_ref=dst,
            send_sem=xin_send.at[a, r - 1],
            recv_sem=xin_recv.at[a, r - 1],
            device_id=dev(x, z),
            device_id_type=MESH,
        ).wait_recv()

    def z_in(d, h, s):
        sign = 1 - 2 * d
        piece = at_z(-sign * (h - 1)) * NX + s
        ref = kv.at[:, pblocks(piece)] if h < half else kv.at[d, pblocks(piece)]
        return pltpu.make_async_remote_copy(
            src_ref=ref,
            dst_ref=ref,
            send_sem=zin_send.at[d, h - 1, s],
            recv_sem=zin_recv.at[d, h - 1, s],
            device_id=dev(x, at_z(sign)),
            device_id_type=MESH,
        )

    def z_in_wait(d, h, s):
        sign = 1 - 2 * d
        piece = at_z(-sign * h) * NX + s
        ref = kv.at[:, pblocks(piece)] if h < half else kv.at[d, pblocks(piece)]
        pltpu.make_async_remote_copy(
            src_ref=ref,
            dst_ref=ref,
            send_sem=zin_send.at[d, h - 1, s],
            recv_sem=zin_recv.at[d, h - 1, s],
            device_id=dev(x, z),
            device_id_type=MESH,
        ).wait_recv()

    for r in (1, 3, 2):
        for a in (0, 1):
            x_in(a, r).start()
    local[0].wait()
    local[1].wait()
    for d in (0, 1):
        z_in(d, 1, x).start()
    for a in (2, 3):
        for r in (2, 1, 3):
            x_in(a, r).start()
    order = (1, 3, 2)
    for r in order:
        for a in (0, 1):
            x_in_wait(a, r)
        for d in (0, 1):
            z_in(d, 1, at_x(-r)).start()
    for h in range(1, half + 1):
        for r in (0,) + order:
            for d in (0, 1):
                z_in_wait(d, h, at_x(-r))
                if h < half:
                    z_in(d, h + 1, at_x(-r)).start()

    ends = []
    total = 0
    for n in range(ndoc):
        total = total + len_ref[n]
        ends.append(total)

    zero = jnp.zeros((C, HD), F32)
    for i in range(NX * per):
        for end in (0, NB + 1):
            ck[i, end] = zero
            cv[i, end] = zero

    local[2].wait()
    local[3].wait()
    for a in (2, 3):
        for r in (2, 1, 3):
            x_in_wait(a, r)

    def place(i):
        s, b = i // per, lax.rem(i, per)
        return span_ref[(s * nz + z) * per + b]

    def x_out(a, r):
        t = at_x(r)
        if a < 2:
            src, dst = (ox, gx)[a].at[prows(t)], (o_out, gq_out)[a].at[:, cols(x, GW)]
        else:
            src, dst = fin.at[a - 2, prows(t)], (gk_out, gv_out)[a - 2].at[:, cols(x, HD)]
        return pltpu.make_async_remote_copy(
            src_ref=src,
            dst_ref=dst,
            send_sem=xout_send.at[a, r - 1],
            recv_sem=xout_recv.at[a, r - 1],
            device_id=dev(t, z),
            device_id_type=MESH,
        )

    def x_out_wait(a, r):
        src = at_x(-r)
        if a < 2:
            dst = (o_out, gq_out)[a].at[:, cols(src, GW)]
        else:
            dst = (gk_out, gv_out)[a - 2].at[:, cols(src, HD)]
        pltpu.make_async_remote_copy(
            src_ref=dst,
            dst_ref=dst,
            send_sem=xout_send.at[a, r - 1],
            recv_sem=xout_recv.at[a, r - 1],
            device_id=dev(x, z),
            device_id_type=MESH,
        ).wait_recv()

    def local_out(a):
        if a < 2:
            src, dst = (ox, gx)[a].at[prows(x)], (o_out, gq_out)[a].at[:, cols(x, GW)]
        else:
            src, dst = fin.at[a - 2, prows(x)], (gk_out, gv_out)[a - 2].at[:, cols(x, HD)]
        return pltpu.make_async_copy(src, dst, loc_sem.at[4 + a])

    scale = HD**-0.5
    lane = lax.broadcasted_iota(jnp.int32, (1, HD), 1)
    row = lax.broadcasted_iota(jnp.int32, (W, HD), 0)

    def block(n, _):
        r = (2, 1, 3, 0)
        rel = jnp.where(n < per, r[0], jnp.where(n < 2 * per, r[1], jnp.where(n < 3 * per, r[2], r[3])))
        i = at_x(rel) * per + lax.rem(n, per)
        at = place(i)
        keys, vals = [], []
        for o in range(NB):
            e = inv_ref[jnp.maximum(at - (NB - 1) + o, 0)]
            keys.append(kv[0, e])
            vals.append(kv[1, e])
        key = jnp.concatenate(keys, axis=0)
        val = jnp.concatenate(vals, axis=0)
        mine = pl.ds(pl.multiple_of(i * C, C), C)
        query = jnp.concatenate([qx[mine, h * HD : (h + 1) * HD] for h in range(GH)], axis=0)
        grad = jnp.concatenate([dx[mine, h * HD : (h + 1) * HD] for h in range(GH)], axis=0)
        pos = at * C + lax.rem(lane, C)
        first = jnp.zeros_like(pos)
        for end in ends:
            first = jnp.where(pos >= end, end, first)
        t = row + (at - (NB - 1)) * C
        seen = jnp.logical_and(t >= first, t <= pos)
        seen = jnp.concatenate([seen] * (GH * C // HD), axis=1)

        def nt(a, b):
            return lax.dot_general(a, b, (((1,), (1,)), ((), ())), preferred_element_type=F32)

        def tn(a, b):
            return lax.dot_general(a, b, (((0,), (0,)), ((), ())), preferred_element_type=F32)

        scores = jnp.where(seen, nt(key, query), -jnp.inf)
        peak = jnp.max(scores, axis=0, keepdims=True)
        weights = jnp.exp2((scores - peak) * (scale * LOG2E))
        probs = weights * (1.0 / jnp.sum(weights, axis=0, keepdims=True))
        low = probs.astype(BF16)
        mixed = tn(val, low).T.astype(BF16)
        grad_probs = nt(val, grad)
        centre = jnp.sum(probs * grad_probs, axis=0, keepdims=True)
        grad_scores = (probs * (grad_probs - centre)).astype(BF16)
        query_grad = (tn(key, grad_scores) * scale).T.astype(BF16)
        for h in range(GH):
            ox[mine, h * HD : (h + 1) * HD] = mixed[h * C : (h + 1) * C]
            gx[mine, h * HD : (h + 1) * HD] = query_grad[h * C : (h + 1) * C]
        key_grad = jnp.dot(grad_scores, query, preferred_element_type=F32) * scale
        val_grad = jnp.dot(low, grad, preferred_element_type=F32)
        ck[i, pl.ds(1, NB)] = key_grad.reshape(NB, C, HD)
        cv[i, pl.ds(1, NB)] = val_grad.reshape(NB, C, HD)

        for m, r_out in enumerate(r[:3]):

            @pl.when(n == (m + 1) * per - 1)
            def _():
                for a in (0, 1):
                    x_out(a, r_out).start()

        return 0

    lax.fori_loop(0, NX * per, block, 0)
    for a in (0, 1):
        local_out(a).start()

    def part(zz, s, b, which):
        at = span_ref[(s * nz + zz) * per + b]
        out = []
        for w in which:
            out.append(jnp.zeros((C, HD), F32))
        for i in range(NX * per):
            o = jnp.minimum(jnp.maximum(at - place(i) + NB, 0), NB + 1)
            for n, w in enumerate(which):
                out[n] = out[n] + (ck, cv)[w][i, o]
        return out

    def z_out(d, h, s):
        sign = 1 - 2 * d
        if h == 1:
            src, dst = send_buf.at[d, h - 1, s, d], recv_buf.at[d, h - 1, s, d]
        else:
            src, dst = send_buf.at[d, h - 1, s], recv_buf.at[d, h - 1, s]
        return pltpu.make_async_remote_copy(
            src_ref=src,
            dst_ref=dst,
            send_sem=zout_send.at[d, h - 1, s],
            recv_sem=zout_recv.at[d, h - 1, s],
            device_id=dev(x, at_z(sign)),
            device_id_type=MESH,
        )

    for h in range(1, half + 1):

        def reduce_step(s, _):
            for d in (0, 1):
                sign = 1 - 2 * d
                owner = at_z(sign * (half + 1 - h))
                which = (d,) if h == 1 else (0, 1)
                if h > 1:
                    z_out(d, h - 1, s).wait_recv()
                for b in range(per):
                    there = pl.ds(b * C, C)
                    for w, sums in zip(which, part(owner, s, b, which)):
                        if h > 2 or (h == 2 and w == d):
                            sums = sums + recv_buf[d, h - 2, s, w, there].astype(F32)
                        send_buf[d, h - 1, s, w, there] = sums.astype(BF16)
                z_out(d, h, s).start()
            return 0

        lax.fori_loop(0, NX, reduce_step, 0)

    def last_step(n, _):
        s = at_x(n + 1)
        for d in (0, 1):
            z_out(d, half, s).wait_recv()
        for b in range(per):
            there = pl.ds(b * C, C)
            for w, sums in enumerate(part(z, s, b, (0, 1))):
                for d in (0, 1):
                    sums = sums + recv_buf[d, half - 1, s, w, there].astype(F32)
                fin[w, pl.ds(pl.multiple_of(s * rows + b * C, C), C)] = sums.astype(BF16)
        for r in (1, 2, 3):

            @pl.when(n == r - 1)
            def _():
                for a in (2, 3):
                    x_out(a, r).start()

        return 0

    lax.fori_loop(0, NX, last_step, 0)
    for a in (2, 3):
        local_out(a).start()

    for a in range(4):
        local_out(a).wait()
        for r in (1, 2, 3):
            x_out_wait(a, r)
            x_out(a, r).wait_send()
            x_in(a, r).wait_send()
    for d in (0, 1):
        for h in range(1, half + 1):
            for s in range(NX):
                z_in(d, h, s).wait_send()
                z_out(d, h, s).wait_send()


def local(queries, keys, values, output_gradient, doc_lengths, span_order):
    nz = lax.axis_size("ctx") // NX
    half = nz // 2
    rows = queries.shape[0]
    per = rows // C
    tokens = rows * NX * nz
    blocks = tokens // C
    places = jnp.arange(blocks, dtype=jnp.int32)
    owner = places // per
    slot = ((owner % nz) * NX + owner // nz) * per + places % per
    inverse = jnp.sum(
        jnp.where(span_order[None, :] == places[:, None], slot[None, :], 0), axis=1, dtype=jnp.int32
    )
    hbm = pl.BlockSpec(memory_space=pl.ANY)
    smem = pl.BlockSpec(memory_space=pltpu.SMEM)
    dma = pltpu.SemaphoreType.DMA
    return pl.pallas_call(
        functools.partial(kernel, nz),
        out_shape=(
            jax.ShapeDtypeStruct(queries.shape, BF16),
            jax.ShapeDtypeStruct(queries.shape, BF16),
            jax.ShapeDtypeStruct(keys.shape, BF16),
            jax.ShapeDtypeStruct(keys.shape, BF16),
        ),
        in_specs=[hbm] * 4 + [smem] * 3,
        out_specs=(hbm,) * 4,
        scratch_shapes=[
            pltpu.VMEM((2, blocks, C, HD), BF16),
            pltpu.VMEM((NX * rows, GW), BF16),
            pltpu.VMEM((NX * rows, GW), BF16),
            pltpu.VMEM((NX * rows, GW), BF16),
            pltpu.VMEM((NX * rows, GW), BF16),
            pltpu.VMEM((NX * per, NB + 2, C, HD), F32),
            pltpu.VMEM((NX * per, NB + 2, C, HD), F32),
            pltpu.VMEM((2, half, NX, 2, rows, HD), BF16),
            pltpu.VMEM((2, half, NX, 2, rows, HD), BF16),
            pltpu.VMEM((2, NX * rows, HD), BF16),
            dma((8,)),
            dma((4, 3)),
            dma((4, 3)),
            dma((2, half, NX)),
            dma((2, half, NX)),
            dma((4, 3)),
            dma((4, 3)),
            dma((2, half, NX)),
            dma((2, half, NX)),
        ],
        compiler_params=pltpu.CompilerParams(
            collective_id=0, has_side_effects=True, vmem_limit_bytes=56 * 2**20
        ),
    )(queries, keys.reshape(per, C, KH * HD), values.reshape(per, C, KH * HD), output_gradient, doc_lengths, span_order, inverse)


def solution(mesh):
    wide = P(("dp", "ctx"), None)
    return jax.shard_map(
        local,
        mesh=mesh,
        in_specs=(wide, wide, wide, wide, P("dp"), P("dp")),
        out_specs=(wide, wide, wide, wide),
        check_vma=False,
    )
```

time: 424 us -> 86.2 us (0.20)
  waiting for transfers between devices: 209 us -> 0 us
  matrix products: 96.5 us -> 0 us
  Pallas kernels: 0 us -> 79.1 us
  starting transfers between devices: 54.2 us -> 0 us
  local copies, waits for them, and re-layouts: 45.8 us -> 5.64 us
  other arithmetic: 14.6 us -> 0.64 us
    all_to_all x8 -> x0, waiting for transfers between devices: 209 us -> none  [the longest x1 44.1 us: local(): lax.all_to_all(key_store, 'ctx', split_axis=0, concat_axis=1, tiled=True)]
    dot_general x56 -> x0, matrix products: 96.5 us -> none  [the longest x16 26.8 us: window_probs(): jnp.dot(query_rows, key_window.T, preferred_element_type=jnp.float32)]
    pallas_call x0 -> x1, Pallas kernels: none -> 79.1 us  [local(): pl.pallas_call(functools.partial(kernel, nz), out_shape=(jax.ShapeDtypeSt...]
    all_to_all x8 -> x0, starting transfers between devices: 54.2 us -> none  [the longest x1 13.2 us: local(): lax.all_to_all(key_spread, 'ctx', split_axis=1, concat_axis=0, tiled=True)]
    gather x8 -> x0, local copies, waits for them, and re-layouts: 15.3 us -> none  [the longest x4 10.5 us: to_storage(): return blocks[span_order].reshape(token_row_count.shape)]
    reduce_sum x19 -> x1, other arithmetic: 9.71 us -> 0.63 us  [local(): jnp.sum(jnp.where(span_order[None, :] == places[:, None], slot[None, :],...]
    all_to_all x4 -> x0, local copies, waits for them, and re-layouts: 6.81 us -> none  [the longest x1 2.27 us: local(): lax.all_to_all(query_store, 'ctx', split_axis=0, concat_axis=1, tiled=True)]
    unnamed x20 -> x12, local copies, waits for them, and re-layouts: 10.6 us -> 5.64 us
  transfers between devices with their start and end apart: 8 -> 0, of which waited for: 7 -> 0; matrix products, arithmetic and copies ran while one was open for 15% -> 0% of each run, Pallas kernels for 0% -> 0%
where the time goes in v1:
time: 86.2 us; the launch traced here: 86 us
  Pallas kernels  79.1 us (92%)
  local copies, waits for them, and re-layouts  5.64 us (7%)
    pallas_call x1, Pallas kernels, local(): pl.pallas_call(functools.partial(kernel, nz), out_shape=(jax.ShapeDtypeSt...  79.1 us
    unnamed x12, local copies, waits for them, and re-layouts  5.64 us

profile of v1, /device:TPU:56, one launch (start us, length us, event | category | flops | bytes accessed | tf_op | source)
XLA Modules:
  0.0 86.0 jit_solution(3939863660633235099)
XLA Ops:
  0.6 0.0 copy-start.3
  0.7 0.6 copy-done.3
  1.3 0.6 select_reduce_fusion.inv_ref
  1.9 79.1 %shard_map.93 = (bf16[128,4096]{1,0:T(8,128)(2,1)}, bf16[128,4096]{1,0:T(8,128)(2,1)}, bf16[128,512]{1,0:T(8,128)(2,1)}, bf16[128,512]{1,0:T(8,128)(2,1)}) custom-call(bf16[128,4096]{1,0:T(8,128)(2,1)} %q_ref.1, bf16[2,64,512]{2,1,0:T(8,128)(2,1)} %bitcast.2, bf16[2,64,512]{2,1,0:T(8,128)(2,1)} %bitcast.3, bf16[128,4096]{1,0:T(8,128)(2,1)} %g_ref.1, ...), custom_call_target="tpu_custom_call" | custom-call | tf_op jit(solution)/shard_map/pallas_call | solution.py:400
  81.0 0.0 copy-start
  81.0 2.4 %copy.14 = bf16[128,4096]{1,0:T(8,128)(2,1)} copy(bf16[128,4096]{1,0:T(8,128)(2,1)} %get-tuple-element.8) | data formatting | bytes 2097152
  83.4 0.0 copy-done
  83.4 0.0 copy-start.2
  83.4 1.0 %copy.15 = bf16[128,4096]{1,0:T(8,128)(2,1)} copy(bf16[128,4096]{1,0:T(8,128)(2,1)S(1)} %copy-done) | data formatting | bytes 2097152
  84.4 0.1 copy-done.2
  84.4 0.0 copy-start.1
  84.4 0.7 copy.16
  85.1 0.3 copy-done.1
  85.4 0.7 copy.17
  (1 shorter events, 0.0 us)
Async XLA Ops:
  0.6 0.7 copy-start.3
  81.0 2.4 %copy-start = (bf16[128,4096]{1,0:T(8,128)(2,1)S(1)}, bf16[128,4096]{1,0:T(8,128)(2,1)}, u32[]{:S(2)}) copy-start(bf16[128,4096]{1,0:T(8,128)(2,1)} %get-tuple-element.9) | copy-start | bytes 3145732
  83.4 1.0 %copy-start.2 = (bf16[128,512]{1,0:T(8,128)(2,1)S(1)}, bf16[128,512]{1,0:T(8,128)(2,1)}, u32[]{:S(2)}) copy-start(bf16[128,512]{1,0:T(8,128)(2,1)} %get-tuple-element.10) | copy-start | bytes 393220
  84.4 1.0 %copy-start.1 = (bf16[128,512]{1,0:T(8,128)(2,1)S(1)}, bf16[128,512]{1,0:T(8,128)(2,1)}, u32[]{:S(2)}) copy-start(bf16[128,512]{1,0:T(8,128)(2,1)} %get-tuple-element.11) | copy-start | bytes 393220

commit v2 on v1

v2 whole, which is shorter than its diff:
```python
import functools

import jax
import jax.numpy as jnp
from jax import lax
from jax.experimental import pallas as pl
from jax.experimental.pallas import tpu as pltpu
from jax.sharding import PartitionSpec as P

HD = 128
QH = 32
KH = 4
GH = QH // KH
C = 64
NB = 7
W = NB * C
NX = 4
GW = GH * HD
LOG2E = 1.4426950408889634
MESH = pl.DeviceIdType.MESH
F32 = jnp.float32
BF16 = jnp.bfloat16


def kernel(
    nz,
    q_ref,
    k_ref,
    v_ref,
    g_ref,
    len_ref,
    span_ref,
    o_out,
    gq_out,
    gk_out,
    gv_out,
    keys,
    vals,
    qx,
    dx,
    ox,
    gx,
    pb,
    ck,
    cv,
    send_buf,
    recv_buf,
    fin,
    inv_row,
    inv_ref,
    loc_sem,
    xin_send,
    xin_recv,
    zin_send,
    zin_recv,
    xout_send,
    xout_recv,
    zout_send,
    zout_recv,
):
    half = nz // 2
    rows = q_ref.shape[0]
    per = rows // C
    kv = (keys, vals)
    blocks = keys.shape[0]
    me = lax.axis_index("ctx")
    x = me // nz
    z = lax.rem(me, nz)

    def at_x(r):
        return lax.rem(x + r + NX, NX)

    def at_z(r):
        return lax.rem(z + r + nz, nz)

    def dev(xx, zz):
        return {"ctx": xx * nz + zz}

    def cols(g, width):
        return pl.ds(pl.multiple_of(g * width, width), width)

    def pblocks(piece):
        return pl.ds(piece * per, per)

    def prows(piece):
        return pl.ds(pl.multiple_of(piece * rows, rows), rows)

    own = z * NX + x
    local = [
        pltpu.make_async_copy(k_ref.at[:, :, cols(x, HD)], keys.at[pblocks(own)], loc_sem.at[0]),
        pltpu.make_async_copy(v_ref.at[:, :, cols(x, HD)], vals.at[pblocks(own)], loc_sem.at[1]),
        pltpu.make_async_copy(q_ref.at[:, cols(x, GW)], qx.at[prows(x)], loc_sem.at[2]),
        pltpu.make_async_copy(g_ref.at[:, cols(x, GW)], dx.at[prows(x)], loc_sem.at[3]),
    ]
    for c in local:
        c.start()

    barrier = pltpu.get_barrier_semaphore()
    peers = [dev(at_x(r), z) for r in (1, 2, 3)] + [dev(x, at_z(r)) for r in (1, -1)]
    for p in peers:
        pl.semaphore_signal(barrier, inc=1, device_id=p, device_id_type=MESH)
    pl.semaphore_wait(barrier, len(peers))

    def x_in(a, r):
        g = at_x(r)
        if a < 2:
            src, dst = (k_ref, v_ref)[a].at[:, :, cols(g, HD)], kv[a].at[pblocks(own)]
        else:
            src, dst = (q_ref, g_ref)[a - 2].at[:, cols(g, GW)], (qx, dx)[a - 2].at[prows(x)]
        return pltpu.make_async_remote_copy(
            src_ref=src,
            dst_ref=dst,
            send_sem=xin_send.at[a, r - 1],
            recv_sem=xin_recv.at[a, r - 1],
            device_id=dev(g, z),
            device_id_type=MESH,
        )

    def x_in_wait(a, r):
        src = at_x(-r)
        if a < 2:
            dst = kv[a].at[pblocks(z * NX + src)]
        else:
            dst = (qx, dx)[a - 2].at[prows(src)]
        pltpu.make_async_remote_copy(
            src_ref=dst,
            dst_ref=dst,
            send_sem=xin_send.at[a, r - 1],
            recv_sem=xin_recv.at[a, r - 1],
            device_id=dev(x, z),
            device_id_type=MESH,
        ).wait_recv()

    def z_in_ref(w, d, h, piece):
        if h < half:
            return kv[w].at[pblocks(piece)]
        return kv[w].at[pl.ds(piece * per + d, 1)]

    def z_in(w, d, h, s):
        sign = 1 - 2 * d
        ref = z_in_ref(w, d, h, at_z(-sign * (h - 1)) * NX + s)
        return pltpu.make_async_remote_copy(
            src_ref=ref,
            dst_ref=ref,
            send_sem=zin_send.at[w, d, h - 1, s],
            recv_sem=zin_recv.at[w, d, h - 1, s],
            device_id=dev(x, at_z(sign)),
            device_id_type=MESH,
        )

    def z_in_wait(w, d, h, s):
        sign = 1 - 2 * d
        ref = z_in_ref(w, d, h, at_z(-sign * h) * NX + s)
        pltpu.make_async_remote_copy(
            src_ref=ref,
            dst_ref=ref,
            send_sem=zin_send.at[w, d, h - 1, s],
            recv_sem=zin_recv.at[w, d, h - 1, s],
            device_id=dev(x, z),
            device_id_type=MESH,
        ).wait_recv()

    order = (0, 1, 3, 2)

    def z_in_pass(w, h, k):
        s = at_x(-order[k])
        for d in (0, 1):
            z_in_wait(w, d, h, s)
            if h < half:
                z_in(w, d, h + 1, s).start()

    def z_in_first(w, k):
        if k > 0:
            x_in_wait(w, order[k])
        for d in (0, 1):
            z_in(w, d, 1, at_x(-order[k])).start()

    for r in (1, 3, 2):
        x_in(0, r).start()
    local[0].wait()
    z_in_first(0, 0)
    for r in (1, 3, 2):
        x_in(1, r).start()
    for a in (2, 3):
        for r in (1, 3):
            x_in(a, r).start()

    at_lane = lax.broadcasted_iota(jnp.int32, inv_row.shape, 1)
    inverse = jnp.zeros(inv_row.shape, jnp.int32)
    for j in range(blocks):
        owner = j // per
        inverse = jnp.where(
            at_lane == span_ref[j], ((owner % nz) * NX + owner // nz) * per + j % per, inverse
        )
    inv_row[...] = inverse
    look = pltpu.make_async_copy(inv_row, inv_ref, loc_sem.at[8])
    look.start()

    for k in (1, 2, 3):
        z_in_first(0, k)
    for h in range(1, half):
        for k in range(NX):
            z_in_pass(0, h, k)

    ends = []
    total = 0
    for n in range(len_ref.shape[0]):
        total = total + len_ref[n]
        ends.append(total)

    zero = jnp.zeros((C, HD), F32)
    for i in range(NX * per):
        for end in (0, NB + 1):
            ck[i, end] = zero
            cv[i, end] = zero

    local[1].wait()
    for k in range(NX):
        z_in_first(1, k)
    for k in range(NX):
        z_in_pass(0, half, k)
    look.wait()
    local[2].wait()
    local[3].wait()

    def place(i):
        s, b = i // per, lax.rem(i, per)
        return span_ref[(s * nz + z) * per + b]

    def x_out(a, r):
        t = at_x(r)
        if a < 2:
            src, dst = (ox, gx)[a].at[prows(t)], (o_out, gq_out)[a].at[:, cols(x, GW)]
        else:
            src, dst = fin.at[a - 2, prows(t)], (gk_out, gv_out)[a - 2].at[:, cols(x, HD)]
        return pltpu.make_async_remote_copy(
            src_ref=src,
            dst_ref=dst,
            send_sem=xout_send.at[a, r - 1],
            recv_sem=xout_recv.at[a, r - 1],
            device_id=dev(t, z),
            device_id_type=MESH,
        )

    def x_out_wait(a, r):
        src = at_x(-r)
        if a < 2:
            dst = (o_out, gq_out)[a].at[:, cols(src, GW)]
        else:
            dst = (gk_out, gv_out)[a - 2].at[:, cols(src, HD)]
        pltpu.make_async_remote_copy(
            src_ref=dst,
            dst_ref=dst,
            send_sem=xout_send.at[a, r - 1],
            recv_sem=xout_recv.at[a, r - 1],
            device_id=dev(x, z),
            device_id_type=MESH,
        ).wait_recv()

    def local_out(a):
        if a < 2:
            src, dst = (ox, gx)[a].at[prows(x)], (o_out, gq_out)[a].at[:, cols(x, GW)]
        else:
            src, dst = fin.at[a - 2, prows(x)], (gk_out, gv_out)[a - 2].at[:, cols(x, HD)]
        return pltpu.make_async_copy(src, dst, loc_sem.at[4 + a])

    def part(w, zz, s, b):
        at = span_ref[(s * nz + zz) * per + b]
        out = None
        for i in range(NX * per):
            o = jnp.minimum(jnp.maximum(at - place(i) + NB, 0), NB + 1)
            term = (ck, cv)[w][i, o]
            out = term if out is None else out + term
        return out

    def z_out(w, d, h, s):
        sign = 1 - 2 * d
        there = (w, d, h - 1, s, d) if h == 1 else (w, d, h - 1, s)
        return pltpu.make_async_remote_copy(
            src_ref=send_buf.at[there],
            dst_ref=recv_buf.at[there],
            send_sem=zout_send.at[w, d, h - 1, s],
            recv_sem=zout_recv.at[w, d, h - 1, s],
            device_id=dev(x, at_z(sign)),
            device_id_type=MESH,
        )

    def pick(n, rels):
        rel = rels[-1]
        for m in range(len(rels) - 2, -1, -1):
            rel = jnp.where(n <= m, rels[m], rel)
        return rel

    def z_out_hop(w, h):
        def step(n, _):
            s = at_x(pick(n, (2, 1, 3, 0)))
            for d in (0, 1):
                sign = 1 - 2 * d
                owner = at_z(sign * (half + 1 - h))
                if h > 1:
                    z_out(w, d, h - 1, s).wait_recv()
                for b in range(per):
                    if h == 1 and b != d:
                        continue
                    sums = part(w, owner, s, b)
                    if h > 2 or (h == 2 and b == d):
                        sums = sums + recv_buf[w, d, h - 2, s, b].astype(F32)
                    send_buf[w, d, h - 1, s, b] = sums.astype(BF16)
                z_out(w, d, h, s).start()
            return 0

        lax.fori_loop(0, NX, step, 0)

    def z_out_last(w):
        def step(n, _):
            s = at_x(pick(n, (2, 1, 3, 0)))
            for d in (0, 1):
                z_out(w, d, half, s).wait_recv()
            for b in range(per):
                sums = part(w, z, s, b)
                for d in (0, 1):
                    sums = sums + recv_buf[w, d, half - 1, s, b].astype(F32)
                fin[w, pl.ds(pl.multiple_of(s * rows + b * C, C), C)] = sums.astype(BF16)
            for m, r in enumerate((2, 1, 3)):

                @pl.when(n == m)
                def _():
                    x_out(2 + w, r).start()

            return 0

        lax.fori_loop(0, NX, step, 0)
        local_out(2 + w).start()

    scale = HD**-0.5
    lane = lax.broadcasted_iota(jnp.int32, (1, HD), 1)
    row = lax.broadcasted_iota(jnp.int32, (W, HD), 0)

    def nt(a, b):
        return lax.dot_general(a, b, (((1,), (1,)), ((), ())), preferred_element_type=F32)

    def tn(a, b):
        return lax.dot_general(a, b, (((0,), (0,)), ((), ())), preferred_element_type=F32)

    def window(w, at):
        found = [kv[w][inv_ref[0, jnp.maximum(at - (NB - 1) + o, 0)]] for o in range(NB)]
        return jnp.concatenate(found, axis=0)

    def stacked(ref, mine):
        return jnp.concatenate([ref[mine, h * HD : (h + 1) * HD] for h in range(GH)], axis=0)

    def unstack(ref, mine, value):
        for h in range(GH):
            ref[mine, h * HD : (h + 1) * HD] = value[h * C : (h + 1) * C]

    def first_half(i):
        at = place(i)
        mine = pl.ds(pl.multiple_of(i * C, C), C)
        pos = at * C + lax.rem(lane, C)
        first = jnp.zeros_like(pos)
        for end in ends:
            first = jnp.where(pos >= end, end, first)
        t = row + (at - (NB - 1)) * C
        seen = jnp.logical_and(t >= first, t <= pos)
        seen = jnp.concatenate([seen] * (GH * C // HD), axis=1)
        scores = jnp.where(seen, nt(window(0, at), stacked(qx, mine)), -jnp.inf)
        peak = jnp.max(scores, axis=0, keepdims=True)
        weights = jnp.exp2((scores - peak) * (scale * LOG2E))
        probs = weights * (1.0 / jnp.sum(weights, axis=0, keepdims=True))
        pb[i] = probs
        val_grad = jnp.dot(probs.astype(BF16), stacked(dx, mine), preferred_element_type=F32)
        cv[i, pl.ds(1, NB)] = val_grad.reshape(NB, C, HD)

    def second_half(i):
        at = place(i)
        mine = pl.ds(pl.multiple_of(i * C, C), C)
        key, val = window(0, at), window(1, at)
        probs = pb[i]
        unstack(ox, mine, tn(val, probs.astype(BF16)).T.astype(BF16))
        grad_probs = nt(val, stacked(dx, mine))
        centre = jnp.sum(probs * grad_probs, axis=0, keepdims=True)
        grad_scores = (probs * (grad_probs - centre)).astype(BF16)
        unstack(gx, mine, (tn(key, grad_scores) * scale).T.astype(BF16))
        key_grad = jnp.dot(grad_scores, stacked(qx, mine), preferred_element_type=F32) * scale
        ck[i, pl.ds(1, NB)] = key_grad.reshape(NB, C, HD)

    near = 3 * per

    def passes(todo):
        for h, k in todo:
            z_in_pass(1, h, k)

    hops = [(h, k) for h in range(1, half + 1) for k in range(NX)]
    cuts = (0, 1, 5, 6, 7, 9, len(hops))

    def step(n, _):
        for m in range(1, near + 1):

            @pl.when(n == m)
            def _():
                passes(hops[cuts[m - 1] : cuts[m]])

        for m, r in ((per, 1), (2 * per, 3), (2 * near, 2)):

            @pl.when(n == m)
            def _():
                for a in (2, 3):
                    x_in_wait(a, r)
                if r != 2:
                    x_in(2 if r == 1 else 3, 2).start()

        @pl.when(n == 2 * near + per)
        def _():
            z_out_hop(1, 1)

        early = n < 2 * near
        stage = jnp.where(early, n // near, (n - 2 * near) // per)
        group = jnp.where(early, lax.rem(n, near) // per, 3)
        i = at_x(-pick(group, (0, 1, 3, 2))) * per + lax.rem(n, per)

        @pl.when(stage == 0)
        def _():
            first_half(i)

        @pl.when(stage == 1)
        def _():
            second_half(i)

        for m, r in ((near + 2 * per, 3), (near + 3 * per, 1), (2 * near + 2 * per, 2)):

            @pl.when(n == m - 1)
            def _():
                for a in (0, 1):
                    x_out(a, r).start()

        return 0

    lax.fori_loop(0, 2 * NX * per, step, 0)
    for a in (0, 1):
        local_out(a).start()
    for h in range(2, half + 1):
        z_out_hop(1, h)
    z_out_hop(0, 1)
    z_out_last(1)
    for h in range(2, half + 1):
        z_out_hop(0, h)
    z_out_last(0)

    for a in range(4):
        local_out(a).wait()
        for r in (1, 2, 3):
            x_out_wait(a, r)
            x_out(a, r).wait_send()
            x_in(a, r).wait_send()
    for w in (0, 1):
        for d in (0, 1):
            for h in range(1, half + 1):
                for s in range(NX):
                    z_in(w, d, h, s).wait_send()
                    z_out(w, d, h, s).wait_send()


def settle(*refs):
    srcs, dsts, sem = refs[:4], refs[4:8], refs[8]
    copies = []
    for n, (src, dst) in enumerate(zip(srcs, dsts)):
        parts = 4 if n < 2 else 1
        count = src.shape[0] // parts
        for m in range(parts):
            there = pl.ds(m * count, count)
            copies.append(pltpu.make_async_copy(src.at[there], dst.at[there], sem.at[n * 4 + m]))
    for c in copies:
        c.start()
    for c in copies:
        c.wait()


def local(queries, keys, values, output_gradient, doc_lengths, span_order):
    nz = lax.axis_size("ctx") // NX
    half = nz // 2
    rows = queries.shape[0]
    per = rows // C
    blocks = per * NX * nz
    hbm = pl.BlockSpec(memory_space=pl.ANY)
    smem = pl.BlockSpec(memory_space=pltpu.SMEM)
    dma = pltpu.SemaphoreType.DMA
    outs = (
        jax.ShapeDtypeStruct(queries.shape, BF16),
        jax.ShapeDtypeStruct(queries.shape, BF16),
        jax.ShapeDtypeStruct(keys.shape, BF16),
        jax.ShapeDtypeStruct(keys.shape, BF16),
    )
    results = pl.pallas_call(
        functools.partial(kernel, nz),
        out_shape=outs,
        in_specs=[hbm] * 4 + [smem] * 2,
        out_specs=(hbm,) * 4,
        scratch_shapes=[
            pltpu.VMEM((blocks, C, HD), BF16),
            pltpu.VMEM((blocks, C, HD), BF16),
            pltpu.VMEM((NX * rows, GW), BF16),
            pltpu.VMEM((NX * rows, GW), BF16),
            pltpu.VMEM((NX * rows, GW), BF16),
            pltpu.VMEM((NX * rows, GW), BF16),
            pltpu.VMEM((NX * per, W, GH * C), F32),
            pltpu.VMEM((NX * per, NB + 2, C, HD), F32),
            pltpu.VMEM((NX * per, NB + 2, C, HD), F32),
            pltpu.VMEM((2, 2, half, NX, per, C, HD), BF16),
            pltpu.VMEM((2, 2, half, NX, per, C, HD), BF16),
            pltpu.VMEM((2, NX * rows, HD), BF16),
            pltpu.VMEM((8, 128), jnp.int32),
            pltpu.SMEM((8, 128), jnp.int32),
            dma((9,)),
            dma((4, 3)),
            dma((4, 3)),
            dma((2, 2, half, NX)),
            dma((2, 2, half, NX)),
            dma((4, 3)),
            dma((4, 3)),
            dma((2, 2, half, NX)),
            dma((2, 2, half, NX)),
        ],
        compiler_params=pltpu.CompilerParams(
            collective_id=0, has_side_effects=True, vmem_limit_bytes=56 * 2**20
        ),
    )(
        queries,
        keys.reshape(per, C, KH * HD),
        values.reshape(per, C, KH * HD),
        output_gradient,
        doc_lengths,
        span_order,
    )
    return pl.pallas_call(
        settle,
        out_shape=outs,
        in_specs=[hbm] * 4,
        out_specs=(hbm,) * 4,
        scratch_shapes=[dma((16,))],
    )(*results)


def solution(mesh):
    wide = P(("dp", "ctx"), None)
    return jax.shard_map(
        local,
        mesh=mesh,
        in_specs=(wide, wide, wide, wide, P("dp"), P("dp")),
        out_specs=(wide, wide, wide, wide),
        check_vma=False,
    )
```

time: 86.2 us -> 161 us (1.87)
  Pallas kernels: 79.1 us -> 161 us
  local copies, waits for them, and re-layouts: 5.64 us -> 0 us
    pallas_call x1 -> x2, Pallas kernels: 79.1 us -> 161 us  [the longest x1 87.9 us: local(): pl.pallas_call(functools.partial(kernel, nz), out_shape=outs, in_specs=[h...]
    unnamed x12 -> x0, local copies, waits for them, and re-layouts: 5.64 us -> none
where the time goes in v2:
time: 161 us
  Pallas kernels  161 us (100%)
    pallas_call x1, Pallas kernels, local(): pl.pallas_call(functools.partial(kernel, nz), out_shape=outs, in_specs=[h...  87.9 us
    pallas_call x1, Pallas kernels, local(): pl.pallas_call(settle, out_shape=outs, in_specs=[hbm] * 4, out_specs=(hbm...  72.7 us

profile of v2, /device:TPU:56, one launch (start us, length us, event | category | flops | bytes accessed | tf_op | source)
XLA Modules:
  0.0 161.3 jit_solution(14821374242669346082)
XLA Ops:
  0.6 87.9 %shard_map.93 = (bf16[128,4096]{1,0:T(8,128)(2,1)}, bf16[128,4096]{1,0:T(8,128)(2,1)}, bf16[128,512]{1,0:T(8,128)(2,1)}, bf16[128,512]{1,0:T(8,128)(2,1)}) custom-call(bf16[128,4096]{1,0:T(8,128)(2,1)} %q_ref.1, bf16[2,64,512]{2,1,0:T(8,128)(2,1)} %bitcast.2, bf16[2,64,512]{2,1,0:T(8,128)(2,1)} %bitcast.3, bf16[128,4096]{1,0:T(8,128)(2,1)} %g_ref.1, ...), custom_call_target="tpu_custom_call" | custom-call | tf_op jit(solution)/shard_map/pallas_call | solution.py:493
  88.6 72.7 %shard_map.94 = (bf16[128,4096]{1,0:T(8,128)(2,1)}, bf16[128,4096]{1,0:T(8,128)(2,1)}, bf16[128,512]{1,0:T(8,128)(2,1)}, bf16[128,512]{1,0:T(8,128)(2,1)}) custom-call(bf16[128,4096]{1,0:T(8,128)(2,1)} %get-tuple-element.8.refs_0_, bf16[128,4096]{1,0:T(8,128)(2,1)} %get-tuple-element.9.refs_1_, bf16[128,512]{1,0:T(8,128)(2,1)} %get-tuple-element.10.refs_2_, ...), custom_call_target="tpu_custom_call" | custom-call | tf_op jit(solution)/shard_map/pallas_call | solution.py:534

commit v3 on v2

v3 whole, which is shorter than its diff:
```python
import functools

import jax
import jax.numpy as jnp
from jax import lax
from jax.experimental import pallas as pl
from jax.experimental.pallas import tpu as pltpu
from jax.sharding import PartitionSpec as P

HD = 128
QH = 32
KH = 4
GH = QH // KH
C = 64
NB = 7
W = NB * C
NX = 4
GW = GH * HD
LOG2E = 1.4426950408889634
MESH = pl.DeviceIdType.MESH
F32 = jnp.float32
BF16 = jnp.bfloat16


def kernel(
    nz,
    q_ref,
    k_ref,
    v_ref,
    g_ref,
    len_ref,
    span_ref,
    o_out,
    gq_out,
    gk_out,
    gv_out,
    kv,
    qx,
    dx,
    ox,
    gx,
    ck,
    cv,
    send_buf,
    recv_buf,
    fin,
    inv_row,
    inv_ref,
    loc_sem,
    xin_send,
    xin_recv,
    zin_send,
    zin_recv,
    xout_send,
    xout_recv,
    zout_send,
    zout_recv,
):
    half = nz // 2
    rows = q_ref.shape[0]
    per = rows // C
    blocks = kv.shape[1]
    me = lax.axis_index("ctx")
    x = me // nz
    z = lax.rem(me, nz)

    def at_x(r):
        return lax.rem(x + r + NX, NX)

    def at_z(r):
        return lax.rem(z + r + nz, nz)

    def dev(xx, zz):
        return {"ctx": xx * nz + zz}

    def cols(g, width):
        return pl.ds(pl.multiple_of(g * width, width), width)

    def pblocks(piece):
        return pl.ds(piece * per, per)

    def prows(piece):
        return pl.ds(pl.multiple_of(piece * rows, rows), rows)

    own = z * NX + x
    local = [
        pltpu.make_async_copy(k_ref.at[:, :, cols(x, HD)], kv.at[0, pblocks(own)], loc_sem.at[0]),
        pltpu.make_async_copy(v_ref.at[:, :, cols(x, HD)], kv.at[1, pblocks(own)], loc_sem.at[1]),
        pltpu.make_async_copy(q_ref.at[:, cols(x, GW)], qx.at[prows(x)], loc_sem.at[2]),
        pltpu.make_async_copy(g_ref.at[:, cols(x, GW)], dx.at[prows(x)], loc_sem.at[3]),
    ]
    for c in local:
        c.start()

    barrier = pltpu.get_barrier_semaphore()
    peers = [dev(at_x(r), z) for r in (1, 2, 3)] + [dev(x, at_z(r)) for r in (1, -1)]
    for p in peers:
        pl.semaphore_signal(barrier, inc=1, device_id=p, device_id_type=MESH)
    pl.semaphore_wait(barrier, len(peers))

    def x_in(a, r):
        g = at_x(r)
        if a < 2:
            src, dst = (k_ref, v_ref)[a].at[:, :, cols(g, HD)], kv.at[a, pblocks(own)]
        else:
            src, dst = (q_ref, g_ref)[a - 2].at[:, cols(g, GW)], (qx, dx)[a - 2].at[prows(x)]
        return pltpu.make_async_remote_copy(
            src_ref=src,
            dst_ref=dst,
            send_sem=xin_send.at[a, r - 1],
            recv_sem=xin_recv.at[a, r - 1],
            device_id=dev(g, z),
            device_id_type=MESH,
        )

    def x_in_wait(a, r):
        src = at_x(-r)
        if a < 2:
            dst = kv.at[a, pblocks(z * NX + src)]
        else:
            dst = (qx, dx)[a - 2].at[prows(src)]
        pltpu.make_async_remote_copy(
            src_ref=dst,
            dst_ref=dst,
            send_sem=xin_send.at[a, r - 1],
            recv_sem=xin_recv.at[a, r - 1],
            device_id=dev(x, z),
            device_id_type=MESH,
        ).wait_recv()

    def z_in_ref(d, h, piece):
        return kv.at[:, pblocks(piece)] if h < half else kv.at[d, pblocks(piece)]

    def z_in(d, h, s):
        sign = 1 - 2 * d
        ref = z_in_ref(d, h, at_z(-sign * (h - 1)) * NX + s)
        return pltpu.make_async_remote_copy(
            src_ref=ref,
            dst_ref=ref,
            send_sem=zin_send.at[d, h - 1, s],
            recv_sem=zin_recv.at[d, h - 1, s],
            device_id=dev(x, at_z(sign)),
            device_id_type=MESH,
        )

    def z_in_wait(d, h, s):
        sign = 1 - 2 * d
        ref = z_in_ref(d, h, at_z(-sign * h) * NX + s)
        pltpu.make_async_remote_copy(
            src_ref=ref,
            dst_ref=ref,
            send_sem=zin_send.at[d, h - 1, s],
            recv_sem=zin_recv.at[d, h - 1, s],
            device_id=dev(x, z),
            device_id_type=MESH,
        ).wait_recv()

    order = (0, 1, 3, 2)

    for r in (1, 3, 2):
        for a in (0, 1):
            x_in(a, r).start()
    local[0].wait()
    local[1].wait()
    for d in (0, 1):
        z_in(d, 1, x).start()
    for r in order[1:]:
        for a in (2, 3):
            x_in(a, r).start()

    at_lane = lax.broadcasted_iota(jnp.int32, inv_row.shape, 1)
    inverse = jnp.zeros(inv_row.shape, jnp.int32)
    for j in range(blocks):
        owner = j // per
        inverse = jnp.where(
            at_lane == span_ref[j], ((owner % nz) * NX + owner // nz) * per + j % per, inverse
        )
    inv_row[...] = inverse
    look = pltpu.make_async_copy(inv_row, inv_ref, loc_sem.at[8])
    look.start()

    for r in order[1:]:
        for a in (0, 1):
            x_in_wait(a, r)
        for d in (0, 1):
            z_in(d, 1, at_x(-r)).start()
    ends = []
    total = 0
    for n in range(len_ref.shape[0]):
        total = total + len_ref[n]
        ends.append(total)

    zero = jnp.zeros((C, HD), F32)
    for i in range(NX * per):
        for end in (0, NB + 1):
            ck[i, end] = zero
            cv[i, end] = zero

    for h in range(1, half + 1):
        for r in order:
            for d in (0, 1):
                z_in_wait(d, h, at_x(-r))
                if h < half:
                    z_in(d, h + 1, at_x(-r)).start()
    look.wait()
    local[2].wait()
    local[3].wait()

    def place(i):
        s, b = i // per, lax.rem(i, per)
        return span_ref[(s * nz + z) * per + b]

    def x_out(a, r):
        t = at_x(r)
        if a < 2:
            src, dst = (ox, gx)[a].at[prows(t)], (o_out, gq_out)[a].at[:, cols(x, GW)]
        else:
            src, dst = fin.at[a - 2, prows(t)], (gk_out, gv_out)[a - 2].at[:, cols(x, HD)]
        return pltpu.make_async_remote_copy(
            src_ref=src,
            dst_ref=dst,
            send_sem=xout_send.at[a, r - 1],
            recv_sem=xout_recv.at[a, r - 1],
            device_id=dev(t, z),
            device_id_type=MESH,
        )

    def x_out_wait(a, r):
        src = at_x(-r)
        if a < 2:
            dst = (o_out, gq_out)[a].at[:, cols(src, GW)]
        else:
            dst = (gk_out, gv_out)[a - 2].at[:, cols(src, HD)]
        pltpu.make_async_remote_copy(
            src_ref=dst,
            dst_ref=dst,
            send_sem=xout_send.at[a, r - 1],
            recv_sem=xout_recv.at[a, r - 1],
            device_id=dev(x, z),
            device_id_type=MESH,
        ).wait_recv()

    def local_out(a):
        if a < 2:
            src, dst = (ox, gx)[a].at[prows(x)], (o_out, gq_out)[a].at[:, cols(x, GW)]
        else:
            src, dst = fin.at[a - 2, prows(x)], (gk_out, gv_out)[a - 2].at[:, cols(x, HD)]
        return pltpu.make_async_copy(src, dst, loc_sem.at[4 + a])

    def part(w, zz, s, b):
        at = span_ref[(s * nz + zz) * per + b]
        out = None
        for i in range(NX * per):
            o = jnp.minimum(jnp.maximum(at - place(i) + NB, 0), NB + 1)
            term = (ck, cv)[w][i, o]
            out = term if out is None else out + term
        return out

    def z_out(d, h, s):
        sign = 1 - 2 * d
        there = (d, h - 1, s, d) if h == 1 else (d, h - 1, s)
        return pltpu.make_async_remote_copy(
            src_ref=send_buf.at[there],
            dst_ref=recv_buf.at[there],
            send_sem=zout_send.at[d, h - 1, s],
            recv_sem=zout_recv.at[d, h - 1, s],
            device_id=dev(x, at_z(sign)),
            device_id_type=MESH,
        )

    def pick(n, rels):
        rel = rels[-1]
        for m in range(len(rels) - 2, -1, -1):
            rel = jnp.where(n <= m, rels[m], rel)
        return rel

    def z_out_hop(h):
        def step(n, _):
            s = at_x(pick(n, (2, 1, 3, 0)))
            for d in (0, 1):
                sign = 1 - 2 * d
                owner = at_z(sign * (half + 1 - h))
                if h > 1:
                    z_out(d, h - 1, s).wait_recv()
                for w in (d,) if h == 1 else (0, 1):
                    for b in range(per):
                        sums = part(w, owner, s, b)
                        if h > 2 or (h == 2 and w == d):
                            sums = sums + recv_buf[d, h - 2, s, w, b].astype(F32)
                        send_buf[d, h - 1, s, w, b] = sums.astype(BF16)
                z_out(d, h, s).start()
            return 0

        lax.fori_loop(0, NX, step, 0)

    def z_out_last():
        def step(n, _):
            s = at_x(pick(n, (2, 1, 3, 0)))
            for d in (0, 1):
                z_out(d, half, s).wait_recv()
            for w in (0, 1):
                for b in range(per):
                    sums = part(w, z, s, b)
                    for d in (0, 1):
                        sums = sums + recv_buf[d, half - 1, s, w, b].astype(F32)
                    fin[w, pl.ds(pl.multiple_of(s * rows + b * C, C), C)] = sums.astype(BF16)
            for m, r in enumerate((2, 1, 3)):

                @pl.when(n == m)
                def _():
                    for a in (2, 3):
                        x_out(a, r).start()

            return 0

        lax.fori_loop(0, NX, step, 0)
        for a in (2, 3):
            local_out(a).start()

    scale = HD**-0.5
    lane = lax.broadcasted_iota(jnp.int32, (1, HD), 1)
    row = lax.broadcasted_iota(jnp.int32, (W, HD), 0)

    def nt(a, b):
        return lax.dot_general(a, b, (((1,), (1,)), ((), ())), preferred_element_type=F32)

    def tn(a, b):
        return lax.dot_general(a, b, (((0,), (0,)), ((), ())), preferred_element_type=F32)

    def window(w, at):
        found = [kv[w, inv_ref[0, jnp.maximum(at - (NB - 1) + o, 0)]] for o in range(NB)]
        return jnp.concatenate(found, axis=0)

    def stacked(ref, mine):
        return jnp.concatenate([ref[mine, h * HD : (h + 1) * HD] for h in range(GH)], axis=0)

    def unstack(ref, mine, value):
        for h in range(GH):
            ref[mine, h * HD : (h + 1) * HD] = value[h * C : (h + 1) * C]

    def block(i):
        at = place(i)
        mine = pl.ds(pl.multiple_of(i * C, C), C)
        pos = at * C + lax.rem(lane, C)
        first = jnp.zeros_like(pos)
        for end in ends:
            first = jnp.where(pos >= end, end, first)
        t = row + (at - (NB - 1)) * C
        seen = jnp.logical_and(t >= first, t <= pos)
        seen = jnp.concatenate([seen] * (GH * C // HD), axis=1)
        key, val = window(0, at), window(1, at)
        query, grad = stacked(qx, mine), stacked(dx, mine)
        scores = jnp.where(seen, nt(key, query), -jnp.inf)
        peak = jnp.max(scores, axis=0, keepdims=True)
        weights = jnp.exp2((scores - peak) * (scale * LOG2E))
        probs = weights * (1.0 / jnp.sum(weights, axis=0, keepdims=True))
        low = probs.astype(BF16)
        unstack(ox, mine, tn(val, low).T.astype(BF16))
        grad_probs = nt(val, grad)
        centre = jnp.sum(probs * grad_probs, axis=0, keepdims=True)
        grad_scores = (probs * (grad_probs - centre)).astype(BF16)
        unstack(gx, mine, (tn(key, grad_scores) * scale).T.astype(BF16))
        key_grad = jnp.dot(grad_scores, query, preferred_element_type=F32) * scale
        val_grad = jnp.dot(low, grad, preferred_element_type=F32)
        ck[i, pl.ds(1, NB)] = key_grad.reshape(NB, C, HD)
        cv[i, pl.ds(1, NB)] = val_grad.reshape(NB, C, HD)

    came = (1, 3, 0, 2)

    def step(n, _):
        for m, r in enumerate(came):
            if r > 0:

                @pl.when(n == m * per)
                def _():
                    for a in (2, 3):
                        x_in_wait(a, r)

        block(at_x(-pick(n // per, came)) * per + lax.rem(n, per))
        for m, r in enumerate(came):
            if r > 0:

                @pl.when(n == (m + 1) * per - 1)
                def _():
                    for a in (0, 1):
                        x_out(a, NX - r).start()

        return 0

    lax.fori_loop(0, NX * per, step, 0)
    for a in (0, 1):
        local_out(a).start()
    for h in range(1, half + 1):
        z_out_hop(h)
    z_out_last()

    for a in range(4):
        local_out(a).wait()
        for r in (1, 2, 3):
            x_out_wait(a, r)
            x_out(a, r).wait_send()
            x_in(a, r).wait_send()
    for d in (0, 1):
        for h in range(1, half + 1):
            for s in range(NX):
                z_in(d, h, s).wait_send()
                z_out(d, h, s).wait_send()


def settle(*refs):
    srcs, dsts, bufs, sem = refs[:4], refs[4:8], refs[8:12], refs[12]
    copies = []
    for n, (src, dst, buf) in enumerate(zip(srcs, dsts, bufs)):
        parts = 4 if n < 2 else 1
        count = src.shape[0] // parts
        for m in range(parts):
            there = pl.ds(m * count, count)
            copies.append(
                (
                    pltpu.make_async_copy(src.at[there], buf.at[there], sem.at[0, n * 4 + m]),
                    pltpu.make_async_copy(buf.at[there], dst.at[there], sem.at[1, n * 4 + m]),
                )
            )
    for into, _ in copies:
        into.start()
    for into, out in copies:
        into.wait()
        out.start()
    for _, out in copies:
        out.wait()


def local(queries, keys, values, output_gradient, doc_lengths, span_order):
    nz = lax.axis_size("ctx") // NX
    half = nz // 2
    rows = queries.shape[0]
    per = rows // C
    blocks = per * NX * nz
    hbm = pl.BlockSpec(memory_space=pl.ANY)
    smem = pl.BlockSpec(memory_space=pltpu.SMEM)
    dma = pltpu.SemaphoreType.DMA
    outs = (
        jax.ShapeDtypeStruct(queries.shape, BF16),
        jax.ShapeDtypeStruct(queries.shape, BF16),
        jax.ShapeDtypeStruct(keys.shape, BF16),
        jax.ShapeDtypeStruct(keys.shape, BF16),
    )
    results = pl.pallas_call(
        functools.partial(kernel, nz),
        out_shape=outs,
        in_specs=[hbm] * 4 + [smem] * 2,
        out_specs=(hbm,) * 4,
        scratch_shapes=[
            pltpu.VMEM((2, blocks, C, HD), BF16),
            pltpu.VMEM((NX * rows, GW), BF16),
            pltpu.VMEM((NX * rows, GW), BF16),
            pltpu.VMEM((NX * rows, GW), BF16),
            pltpu.VMEM((NX * rows, GW), BF16),
            pltpu.VMEM((NX * per, NB + 2, C, HD), F32),
            pltpu.VMEM((NX * per, NB + 2, C, HD), F32),
            pltpu.VMEM((2, half, NX, 2, per, C, HD), BF16),
            pltpu.VMEM((2, half, NX, 2, per, C, HD), BF16),
            pltpu.VMEM((2, NX * rows, HD), BF16),
            pltpu.VMEM((8, 128), jnp.int32),
            pltpu.SMEM((8, 128), jnp.int32),
            dma((9,)),
            dma((4, 3)),
            dma((4, 3)),
            dma((2, half, NX)),
            dma((2, half, NX)),
            dma((4, 3)),
            dma((4, 3)),
            dma((2, half, NX)),
            dma((2, half, NX)),
        ],
        compiler_params=pltpu.CompilerParams(
            collective_id=0, has_side_effects=True, vmem_limit_bytes=56 * 2**20
        ),
    )(
        queries,
        keys.reshape(per, C, KH * HD),
        values.reshape(per, C, KH * HD),
        output_gradient,
        doc_lengths,
        span_order,
    )
    return pl.pallas_call(
        settle,
        out_shape=outs,
        in_specs=[hbm] * 4,
        out_specs=(hbm,) * 4,
        scratch_shapes=[pltpu.VMEM(o.shape, o.dtype) for o in outs] + [dma((2, 16))],
    )(*results)


def solution(mesh):
    wide = P(("dp", "ctx"), None)
    return jax.shard_map(
        local,
        mesh=mesh,
        in_specs=(wide, wide, wide, wide, P("dp"), P("dp")),
        out_specs=(wide, wide, wide, wide),
        check_vma=False,
    )
```

time: 161 us -> 77.4 us (0.48)
  Pallas kernels: 161 us -> 76.6 us
    pallas_call x1, Pallas kernels: 72.7 us -> 2.62 us  [local(): pl.pallas_call(settle, out_shape=outs, in_specs=[hbm] * 4, out_specs=(hbm...]
    pallas_call x1, Pallas kernels: 87.9 us -> 74 us  [local(): pl.pallas_call(functools.partial(kernel, nz), out_shape=outs, in_specs=[h...]
where the time goes in v3:
time: 77.4 us; the launch traced here: 77.2 us
  Pallas kernels  76.6 us (99%)
    pallas_call x1, Pallas kernels, local(): pl.pallas_call(functools.partial(kernel, nz), out_shape=outs, in_specs=[h...  74 us
    pallas_call x1, Pallas kernels, local(): pl.pallas_call(settle, out_shape=outs, in_specs=[hbm] * 4, out_specs=(hbm...  2.62 us

profile of v3, /device:TPU:56, one launch (start us, length us, event | category | flops | bytes accessed | tf_op | source)
XLA Modules:
  0.0 77.2 jit_solution(13111117188022597839)
XLA Ops:
  0.6 74.0 %shard_map.93 = (bf16[128,4096]{1,0:T(8,128)(2,1)}, bf16[128,4096]{1,0:T(8,128)(2,1)}, bf16[128,512]{1,0:T(8,128)(2,1)}, bf16[128,512]{1,0:T(8,128)(2,1)}) custom-call(bf16[128,4096]{1,0:T(8,128)(2,1)} %q_ref.1, bf16[2,64,512]{2,1,0:T(8,128)(2,1)} %bitcast.2, bf16[2,64,512]{2,1,0:T(8,128)(2,1)} %bitcast.3, bf16[128,4096]{1,0:T(8,128)(2,1)} %g_ref.1, ...), custom_call_target="tpu_custom_call" | custom-call | tf_op jit(solution)/shard_map/pallas_call | solution.py:448
  74.6 2.6 %shard_map.94 = (bf16[128,4096]{1,0:T(8,128)(2,1)}, bf16[128,4096]{1,0:T(8,128)(2,1)}, bf16[128,512]{1,0:T(8,128)(2,1)}, bf16[128,512]{1,0:T(8,128)(2,1)}) custom-call(bf16[128,4096]{1,0:T(8,128)(2,1)} %get-tuple-element.8.refs_0_, bf16[128,4096]{1,0:T(8,128)(2,1)} %get-tuple-element.9.refs_1_, bf16[128,512]{1,0:T(8,128)(2,1)} %get-tuple-element.10.refs_2_, ...), custom_call_target="tpu_custom_call" | custom-call | tf_op jit(solution)/shard_map/pallas_call | solution.py:487

commit v4 on v3

--- a/solution.py
+++ b/solution.py
@@ -17,6 +17,8 @@
 NX = 4
 GW = GH * HD
 LOG2E = 1.4426950408889634
+STAGES = 8
+LAG = 3
 MESH = pl.DeviceIdType.MESH
 F32 = jnp.float32
 BF16 = jnp.bfloat16
@@ -179,11 +181,24 @@
     look = pltpu.make_async_copy(inv_row, inv_ref, loc_sem.at[8])
     look.start()
 
-    for r in order[1:]:
+    def z_in_first(r):
         for a in (0, 1):
             x_in_wait(a, r)
         for d in (0, 1):
             z_in(d, 1, at_x(-r)).start()
+
+    def z_in_pass(h, r):
+        for d in (0, 1):
+            z_in_wait(d, h, at_x(-r))
+            if h < half:
+                z_in(d, h + 1, at_x(-r)).start()
+
+    z_in_pass(1, 0)
+    z_in_first(1)
+    z_in_first(3)
+    z_in_pass(2, 0)
+    z_in_first(2)
+
     ends = []
     total = 0
     for n in range(len_ref.shape[0]):
@@ -198,10 +213,8 @@
 
     for h in range(1, half + 1):
         for r in order:
-            for d in (0, 1):
-                z_in_wait(d, h, at_x(-r))
-                if h < half:
-                    z_in(d, h + 1, at_x(-r)).start()
+            if r > 0 or h > 2:
+                z_in_pass(h, r)
     look.wait()
     local[2].wait()
     local[3].wait()
@@ -350,20 +363,35 @@
         seen = jnp.concatenate([seen] * (GH * C // HD), axis=1)
         key, val = window(0, at), window(1, at)
         query, grad = stacked(qx, mine), stacked(dx, mine)
-        scores = jnp.where(seen, nt(key, query), -jnp.inf)
+        scores = nt(key, query)
+        yield
+        grad_probs = nt(val, grad)
+        yield
+        scores = jnp.where(seen, scores, -jnp.inf)
         peak = jnp.max(scores, axis=0, keepdims=True)
         weights = jnp.exp2((scores - peak) * (scale * LOG2E))
         probs = weights * (1.0 / jnp.sum(weights, axis=0, keepdims=True))
         low = probs.astype(BF16)
+        yield
+        val_grad = jnp.dot(low, grad, preferred_element_type=F32)
+        cv[i, pl.ds(1, NB)] = val_grad.reshape(NB, C, HD)
+        yield
         unstack(ox, mine, tn(val, low).T.astype(BF16))
-        grad_probs = nt(val, grad)
+        yield
         centre = jnp.sum(probs * grad_probs, axis=0, keepdims=True)
         grad_scores = (probs * (grad_probs - centre)).astype(BF16)
+        yield
         unstack(gx, mine, (tn(key, grad_scores) * scale).T.astype(BF16))
+        yield
         key_grad = jnp.dot(grad_scores, query, preferred_element_type=F32) * scale
-        val_grad = jnp.dot(low, grad, preferred_element_type=F32)
         ck[i, pl.ds(1, NB)] = key_grad.reshape(NB, C, HD)
-        cv[i, pl.ds(1, NB)] = val_grad.reshape(NB, C, HD)
+
+    def group(src):
+        todo = [block(src * per + b) for b in range(per)]
+        for t in range(STAGES + LAG * (per - 1)):
+            for b in range(per):
+                if t >= LAG * b:
+                    next(todo[b], None)
 
     came = (1, 3, 0, 2)
 
@@ -371,23 +399,23 @@
         for m, r in enumerate(came):
             if r > 0:
 
-                @pl.when(n == m * per)
+                @pl.when(n == m)
                 def _():
                     for a in (2, 3):
                         x_in_wait(a, r)
 
-        block(at_x(-pick(n // per, came)) * per + lax.rem(n, per))
+        group(at_x(-pick(n, came)))
         for m, r in enumerate(came):
             if r > 0:
 
-                @pl.when(n == (m + 1) * per - 1)
+                @pl.when(n == m)
                 def _():
                     for a in (0, 1):
                         x_out(a, NX - r).start()
 
         return 0
 
-    lax.fori_loop(0, NX * per, step, 0)
+    lax.fori_loop(0, NX, step, 0)
     for a in (0, 1):
         local_out(a).start()
     for h in range(1, half + 1):

time: 77.4 us -> 72.9 us (0.942)
  Pallas kernels: 76.6 us -> 72.1 us
    pallas_call x1, Pallas kernels: 74 us -> 69.5 us  [local(): pl.pallas_call(functools.partial(kernel, nz), out_shape=outs, in_specs=[h...]
where the time goes in v4:
time: 72.9 us; the launch traced here: 72.8 us
  Pallas kernels  72.1 us (99%)
    pallas_call x1, Pallas kernels, local(): pl.pallas_call(functools.partial(kernel, nz), out_shape=outs, in_specs=[h...  69.5 us
    pallas_call x1, Pallas kernels, local(): pl.pallas_call(settle, out_shape=outs, in_specs=[hbm] * 4, out_specs=(hbm...  2.62 us

profile of v4, /device:TPU:56, one launch (start us, length us, event | category | flops | bytes accessed | tf_op | source)
XLA Modules:
  0.0 72.8 jit_solution(8106622767805391262)
XLA Ops:
  0.6 69.5 %shard_map.93 = (bf16[128,4096]{1,0:T(8,128)(2,1)}, bf16[128,4096]{1,0:T(8,128)(2,1)}, bf16[128,512]{1,0:T(8,128)(2,1)}, bf16[128,512]{1,0:T(8,128)(2,1)}) custom-call(bf16[128,4096]{1,0:T(8,128)(2,1)} %q_ref.1, bf16[2,64,512]{2,1,0:T(8,128)(2,1)} %bitcast.2, bf16[2,64,512]{2,1,0:T(8,128)(2,1)} %bitcast.3, bf16[128,4096]{1,0:T(8,128)(2,1)} %g_ref.1, ...), custom_call_target="tpu_custom_call" | custom-call | tf_op jit(solution)/shard_map/pallas_call | solution.py:476
  70.1 2.6 %shard_map.94 = (bf16[128,4096]{1,0:T(8,128)(2,1)}, bf16[128,4096]{1,0:T(8,128)(2,1)}, bf16[128,512]{1,0:T(8,128)(2,1)}, bf16[128,512]{1,0:T(8,128)(2,1)}) custom-call(bf16[128,4096]{1,0:T(8,128)(2,1)} %get-tuple-element.8.refs_0_, bf16[128,4096]{1,0:T(8,128)(2,1)} %get-tuple-element.9.refs_1_, bf16[128,512]{1,0:T(8,128)(2,1)} %get-tuple-element.10.refs_2_, ...), custom_call_target="tpu_custom_call" | custom-call | tf_op jit(solution)/shard_map/pallas_call | solution.py:515

commit v5 on v4

--- a/solution.py
+++ b/solution.py
@@ -30,8 +30,8 @@
     k_ref,
     v_ref,
     g_ref,
-    len_ref,
-    span_ref,
+    len_hbm,
+    span_hbm,
     o_out,
     gq_out,
     gk_out,
@@ -46,6 +46,8 @@
     send_buf,
     recv_buf,
     fin,
+    len_ref,
+    span_ref,
     inv_row,
     inv_ref,
     loc_sem,
@@ -91,6 +93,8 @@
         pltpu.make_async_copy(q_ref.at[:, cols(x, GW)], qx.at[prows(x)], loc_sem.at[2]),
         pltpu.make_async_copy(g_ref.at[:, cols(x, GW)], dx.at[prows(x)], loc_sem.at[3]),
     ]
+    local.append(pltpu.make_async_copy(len_hbm, len_ref, loc_sem.at[9]))
+    local.append(pltpu.make_async_copy(span_hbm, span_ref, loc_sem.at[10]))
     for c in local:
         c.start()
 
@@ -170,6 +174,8 @@
         for a in (2, 3):
             x_in(a, r).start()
 
+    local[4].wait()
+    local[5].wait()
     at_lane = lax.broadcasted_iota(jnp.int32, inv_row.shape, 1)
     inverse = jnp.zeros(inv_row.shape, jnp.int32)
     for j in range(blocks):
@@ -293,14 +299,14 @@
             for d in (0, 1):
                 sign = 1 - 2 * d
                 owner = at_z(sign * (half + 1 - h))
+                which = [(w, b) for w in ((d,) if h == 1 else (0, 1)) for b in range(per)]
+                parts = [part(w, owner, s, b) for w, b in which]
                 if h > 1:
                     z_out(d, h - 1, s).wait_recv()
-                for w in (d,) if h == 1 else (0, 1):
-                    for b in range(per):
-                        sums = part(w, owner, s, b)
-                        if h > 2 or (h == 2 and w == d):
-                            sums = sums + recv_buf[d, h - 2, s, w, b].astype(F32)
-                        send_buf[d, h - 1, s, w, b] = sums.astype(BF16)
+                for (w, b), sums in zip(which, parts):
+                    if h > 2 or (h == 2 and w == d):
+                        sums = sums + recv_buf[d, h - 2, s, w, b].astype(F32)
+                    send_buf[d, h - 1, s, w, b] = sums.astype(BF16)
                 z_out(d, h, s).start()
             return 0
 
@@ -309,14 +315,14 @@
     def z_out_last():
         def step(n, _):
             s = at_x(pick(n, (2, 1, 3, 0)))
+            which = [(w, b) for w in (0, 1) for b in range(per)]
+            parts = [part(w, z, s, b) for w, b in which]
             for d in (0, 1):
                 z_out(d, half, s).wait_recv()
-            for w in (0, 1):
-                for b in range(per):
-                    sums = part(w, z, s, b)
-                    for d in (0, 1):
-                        sums = sums + recv_buf[d, half - 1, s, w, b].astype(F32)
-                    fin[w, pl.ds(pl.multiple_of(s * rows + b * C, C), C)] = sums.astype(BF16)
+            for (w, b), sums in zip(which, parts):
+                for d in (0, 1):
+                    sums = sums + recv_buf[d, half - 1, s, w, b].astype(F32)
+                fin[w, pl.ds(pl.multiple_of(s * rows + b * C, C), C)] = sums.astype(BF16)
             for m, r in enumerate((2, 1, 3)):
 
                 @pl.when(n == m)
@@ -436,26 +442,14 @@
 
 
 def settle(*refs):
-    srcs, dsts, bufs, sem = refs[:4], refs[4:8], refs[8:12], refs[12]
-    copies = []
-    for n, (src, dst, buf) in enumerate(zip(srcs, dsts, bufs)):
-        parts = 4 if n < 2 else 1
-        count = src.shape[0] // parts
-        for m in range(parts):
-            there = pl.ds(m * count, count)
-            copies.append(
-                (
-                    pltpu.make_async_copy(src.at[there], buf.at[there], sem.at[0, n * 4 + m]),
-                    pltpu.make_async_copy(buf.at[there], dst.at[there], sem.at[1, n * 4 + m]),
-                )
-            )
-    for into, _ in copies:
-        into.start()
-    for into, out in copies:
-        into.wait()
-        out.start()
-    for _, out in copies:
-        out.wait()
+    srcs, dsts, sem = refs[:4], refs[4:8], refs[8]
+    copies = [
+        pltpu.make_async_copy(src, dst, sem.at[n]) for n, (src, dst) in enumerate(zip(srcs, dsts))
+    ]
+    for c in copies:
+        c.start()
+    for c in copies:
+        c.wait()
 
 
 def local(queries, keys, values, output_gradient, doc_lengths, span_order):
@@ -465,7 +459,6 @@
     per = rows // C
     blocks = per * NX * nz
     hbm = pl.BlockSpec(memory_space=pl.ANY)
-    smem = pl.BlockSpec(memory_space=pltpu.SMEM)
     dma = pltpu.SemaphoreType.DMA
     outs = (
         jax.ShapeDtypeStruct(queries.shape, BF16),
@@ -475,9 +468,9 @@
     )
     results = pl.pallas_call(
         functools.partial(kernel, nz),
-        out_shape=outs,
-        in_specs=[hbm] * 4 + [smem] * 2,
-        out_specs=(hbm,) * 4,
+        out_shape=tuple(pltpu.VMEM(o.shape, o.dtype) for o in outs),
+        in_specs=[hbm] * 6,
+        out_specs=(pl.BlockSpec(memory_space=pltpu.VMEM),) * 4,
         scratch_shapes=[
             pltpu.VMEM((2, blocks, C, HD), BF16),
             pltpu.VMEM((NX * rows, GW), BF16),
@@ -489,9 +482,11 @@
             pltpu.VMEM((2, half, NX, 2, per, C, HD), BF16),
             pltpu.VMEM((2, half, NX, 2, per, C, HD), BF16),
             pltpu.VMEM((2, NX * rows, HD), BF16),
+            pltpu.SMEM(doc_lengths.shape, jnp.int32),
+            pltpu.SMEM(span_order.shape, jnp.int32),
             pltpu.VMEM((8, 128), jnp.int32),
             pltpu.SMEM((8, 128), jnp.int32),
-            dma((9,)),
+            dma((11,)),
             dma((4, 3)),
             dma((4, 3)),
             dma((2, half, NX)),
@@ -517,8 +512,8 @@
         out_shape=outs,
         in_specs=[hbm] * 4,
         out_specs=(hbm,) * 4,
-        scratch_shapes=[pltpu.VMEM(o.shape, o.dtype) for o in outs] + [dma((2, 16))],
-    )(*results)
+        scratch_shapes=[dma((4,))],
+    )(*(pltpu.with_memory_space_constraint(r, pltpu.VMEM) for r in results))
 
 
 def solution(mesh):

time: 72.9 us -> 70.7 us (0.970)
  Pallas kernels: 72.1 us -> 69.9 us
    pallas_call x1, Pallas kernels: 2.62 us -> 1.43 us  [local(): pl.pallas_call(settle, out_shape=outs, in_specs=[hbm] * 4, out_specs=(hbm...]
    pallas_call x1, Pallas kernels: 69.5 us -> 68.5 us  [local(): pl.pallas_call(functools.partial(kernel, nz), out_shape=tuple((pltpu.VMEM...]
where the time goes in v5:
time: 70.7 us; the launch traced here: 70.5 us
  Pallas kernels  69.9 us (99%)
    pallas_call x1, Pallas kernels, local(): pl.pallas_call(functools.partial(kernel, nz), out_shape=tuple((pltpu.VMEM...  68.5 us
    pallas_call x1, Pallas kernels, local(): pl.pallas_call(settle, out_shape=outs, in_specs=[hbm] * 4, out_specs=(hbm...  1.43 us

profile of v5, /device:TPU:56, one launch (start us, length us, event | category | flops | bytes accessed | tf_op | source)
XLA Modules:
  0.0 70.5 jit_solution(11794795421434985986)
XLA Ops:
  0.6 68.5 %shard_map.93 = (bf16[128,4096]{1,0:T(8,128)(2,1)S(1)}, bf16[128,4096]{1,0:T(8,128)(2,1)S(1)}, bf16[128,512]{1,0:T(8,128)(2,1)S(1)}, bf16[128,512]{1,0:T(8,128)(2,1)S(1)}) custom-call(bf16[128,4096]{1,0:T(8,128)(2,1)} %q_ref.1, bf16[2,64,512]{2,1,0:T(8,128)(2,1)} %bitcast.2, bf16[2,64,512]{2,1,0:T(8,128)(2,1)} %bitcast.3, bf16[128,4096]{1,0:T(8,128)(2,1)} %g_ref.1, ...), custom_call_target="tpu_custom_call" | custom-call | tf_op jit(solution)/shard_map/pallas_call | solution.py:469
  69.1 1.4 %shard_map.94 = (bf16[128,4096]{1,0:T(8,128)(2,1)}, bf16[128,4096]{1,0:T(8,128)(2,1)}, bf16[128,512]{1,0:T(8,128)(2,1)}, bf16[128,512]{1,0:T(8,128)(2,1)}) custom-call(bf16[128,4096]{1,0:T(8,128)(2,1)S(1)} %get-tuple-element.8.refs_0_, bf16[128,4096]{1,0:T(8,128)(2,1)S(1)} %get-tuple-element.9.refs_1_, bf16[128,512]{1,0:T(8,128)(2,1)S(1)} %get-tuple-element.10.refs_2_, ...), custom_call_target="tpu_custom_call" | custom-call | tf_op jit(solution)/shard_map/pallas_call | solution.py:510

commit v6 on v5

--- a/solution.py
+++ b/solution.py
@@ -17,8 +17,6 @@
 NX = 4
 GW = GH * HD
 LOG2E = 1.4426950408889634
-STAGES = 8
-LAG = 3
 MESH = pl.DeviceIdType.MESH
 F32 = jnp.float32
 BF16 = jnp.bfloat16
@@ -43,6 +41,8 @@
     gx,
     ck,
     cv,
+    low_buf,
+    score_buf,
     send_buf,
     recv_buf,
     fin,
@@ -357,7 +357,7 @@
         for h in range(GH):
             ref[mine, h * HD : (h + 1) * HD] = value[h * C : (h + 1) * C]
 
-    def block(i):
+    def block(i, late):
         at = place(i)
         mine = pl.ds(pl.multiple_of(i * C, C), C)
         pos = at * C + lax.rem(lane, C)
@@ -378,53 +378,80 @@
         weights = jnp.exp2((scores - peak) * (scale * LOG2E))
         probs = weights * (1.0 / jnp.sum(weights, axis=0, keepdims=True))
         low = probs.astype(BF16)
+        if late:
+            low_buf[i] = low
         yield
         val_grad = jnp.dot(low, grad, preferred_element_type=F32)
         cv[i, pl.ds(1, NB)] = val_grad.reshape(NB, C, HD)
         yield
-        unstack(ox, mine, tn(val, low).T.astype(BF16))
-        yield
+        if not late:
+            unstack(ox, mine, tn(val, low).T.astype(BF16))
+            yield
         centre = jnp.sum(probs * grad_probs, axis=0, keepdims=True)
         grad_scores = (probs * (grad_probs - centre)).astype(BF16)
+        if late:
+            score_buf[i] = grad_scores
         yield
-        unstack(gx, mine, (tn(key, grad_scores) * scale).T.astype(BF16))
-        yield
+        if not late:
+            unstack(gx, mine, (tn(key, grad_scores) * scale).T.astype(BF16))
+            yield
         key_grad = jnp.dot(grad_scores, query, preferred_element_type=F32) * scale
         ck[i, pl.ds(1, NB)] = key_grad.reshape(NB, C, HD)
 
-    def group(src):
-        todo = [block(src * per + b) for b in range(per)]
-        for t in range(STAGES + LAG * (per - 1)):
+    def finish(i):
+        at = place(i)
+        mine = pl.ds(pl.multiple_of(i * C, C), C)
+        unstack(ox, mine, tn(window(1, at), low_buf[i]).T.astype(BF16))
+        yield
+        unstack(gx, mine, (tn(window(0, at), score_buf[i]) * scale).T.astype(BF16))
+
+    def group(src, work, lag):
+        todo = [work(src * per + b) for b in range(per)]
+        busy = [True] * per
+        t = 0
+        while any(busy):
             for b in range(per):
-                if t >= LAG * b:
-                    next(todo[b], None)
-
-    came = (1, 3, 0, 2)
-
-    def step(n, _):
-        for m, r in enumerate(came):
-            if r > 0:
-
-                @pl.when(n == m)
-                def _():
-                    for a in (2, 3):
-                        x_in_wait(a, r)
-
-        group(at_x(-pick(n, came)))
-        for m, r in enumerate(came):
-            if r > 0:
-
-                @pl.when(n == m)
-                def _():
-                    for a in (0, 1):
-                        x_out(a, NX - r).start()
-
+                if busy[b] and t >= lag * b:
+                    busy[b] = next(todo[b], "end") != "end"
+            t += 1
+
+    def arrive(n, m, r):
+        @pl.when(n == m)
+        def _():
+            for a in (2, 3):
+                x_in_wait(a, r)
+
+    def leave(n, m, r):
+        @pl.when(n == m)
+        def _():
+            for a in (0, 1):
+                x_out(a, r).start()
+
+    def near(n, _):
+        arrive(n, 0, 1)
+        arrive(n, 1, 3)
+        group(at_x(-pick(n, (1, 3))), functools.partial(block, late=False), 3)
+        leave(n, 0, 3)
+        leave(n, 1, 1)
         return 0
 
-    lax.fori_loop(0, NX, step, 0)
+    def far(n, _):
+        arrive(n, 1, 2)
+        group(at_x(-pick(n, (0, 2))), functools.partial(block, late=True), 2)
+        return 0
+
+    def rest(n, _):
+        group(at_x(-pick(n, (2, 0))), finish, 1)
+        leave(n, 0, 2)
+        return 0
+
+    lax.fori_loop(0, 2, near, 0)
+    lax.fori_loop(0, 2, far, 0)
+    z_out_hop(1)
+    lax.fori_loop(0, 2, rest, 0)
     for a in (0, 1):
         local_out(a).start()
-    for h in range(1, half + 1):
+    for h in range(2, half + 1):
         z_out_hop(h)
     z_out_last()
 
@@ -479,6 +506,8 @@
             pltpu.VMEM((NX * rows, GW), BF16),
             pltpu.VMEM((NX * per, NB + 2, C, HD), F32),
             pltpu.VMEM((NX * per, NB + 2, C, HD), F32),
+            pltpu.VMEM((NX * per, W, GH * C), BF16),
+            pltpu.VMEM((NX * per, W, GH * C), BF16),
             pltpu.VMEM((2, half, NX, 2, per, C, HD), BF16),
             pltpu.VMEM((2, half, NX, 2, per, C, HD), BF16),
             pltpu.VMEM((2, NX * rows, HD), BF16),

time: 70.7 us -> 70.1 us (level)
  no operation moved by 1% of the time
where the time goes in v6:
time: 70.1 us; the launch traced here: 70 us
  Pallas kernels  69.3 us (99%)
    pallas_call x1, Pallas kernels, local(): pl.pallas_call(functools.partial(kernel, nz), out_shape=tuple((pltpu.VMEM...  67.9 us
    pallas_call x1, Pallas kernels, local(): pl.pallas_call(settle, out_shape=outs, in_specs=[hbm] * 4, out_specs=(hbm...  1.43 us

profile of v6, /device:TPU:56, one launch (start us, length us, event | category | flops | bytes accessed | tf_op | source)
XLA Modules:
  0.0 70.0 jit_solution(1985861435017140058)
XLA Ops:
  0.6 67.9 %shard_map.93 = (bf16[128,4096]{1,0:T(8,128)(2,1)S(1)}, bf16[128,4096]{1,0:T(8,128)(2,1)S(1)}, bf16[128,512]{1,0:T(8,128)(2,1)S(1)}, bf16[128,512]{1,0:T(8,128)(2,1)S(1)}) custom-call(bf16[128,4096]{1,0:T(8,128)(2,1)} %q_ref.1, bf16[2,64,512]{2,1,0:T(8,128)(2,1)} %bitcast.2, bf16[2,64,512]{2,1,0:T(8,128)(2,1)} %bitcast.3, bf16[128,4096]{1,0:T(8,128)(2,1)} %g_ref.1, ...), custom_call_target="tpu_custom_call" | custom-call | tf_op jit(solution)/shard_map/pallas_call | solution.py:496
  68.5 1.4 %shard_map.94 = (bf16[128,4096]{1,0:T(8,128)(2,1)}, bf16[128,4096]{1,0:T(8,128)(2,1)}, bf16[128,512]{1,0:T(8,128)(2,1)}, bf16[128,512]{1,0:T(8,128)(2,1)}) custom-call(bf16[128,4096]{1,0:T(8,128)(2,1)S(1)} %get-tuple-element.8.refs_0_, bf16[128,4096]{1,0:T(8,128)(2,1)S(1)} %get-tuple-element.9.refs_1_, bf16[128,512]{1,0:T(8,128)(2,1)S(1)} %get-tuple-element.10.refs_2_, ...), custom_call_target="tpu_custom_call" | custom-call | tf_op jit(solution)/shard_map/pallas_call | solution.py:539
